TPU v7x, 256 devices: a whole 4x4x8 slice. The times are simulated.
256 devices in a mesh: kvh: 8 (over x, core), store: 32 (over y, z).
Axes of the slice: x: 4, y: 4, z: 8, core: 2. Of those that a mesh axis runs over, the one named last changes fastest.
Arguments:
- query_heads: bfloat16 [1024, 8, 8, 128], P('store', 'kvh'), may hold values from -1024 to 1024
- span_keys: bfloat16 [512, 8, 512, 128], P('store', 'kvh'), may hold values from -4 to 4
- span_values: bfloat16 [512, 8, 512, 128], P('store', 'kvh'), may hold values from -6 to 6
- cited_spans: int32 [1024, 32], P('store'), may hold values from 0 to 511, as said below
- cite_count: int32 [1024], P('store'), may hold values from 8 to 32, as said below
- out_weight: bfloat16 [8192, 8192], P('kvh', 'store'), may hold values from -0.0625 to 0.0625
Outputs:
- mixed: bfloat16 [1024, 8192], P('kvh', 'store')
Inputs may be any that keep to these rules, and one draw needn't show every extreme that they name: `cited_spans`: the first cite_count[r] entries of a row are distinct span ids; the later entries are ids of spans cited by rows of the same store index and are not read. Among the entries that are read, the rows of one store index cite exactly 2 distinct spans of each store shard (span c is held by store index c // 16). `cite_count`: the first row of each store index cites 32 spans.
All inputs are finite; a program needn't handle non-finite values.
Results may differ from a plain program's by a relative error of at most 0.005.
Values may be sent and summed in bfloat16 or wider, within the bound.
No kernel may reach another device: no remote copies, remote signals or barrier semaphores. Data moves between devices by JAX's collectives and lax.ppermute only.
A program may use at most 128 MiB of HBM per device.

v0:
```python
import jax
import jax.numpy as jnp
from jax import lax
from jax.sharding import PartitionSpec as P

POOL = 64


def per_device(query_heads, span_keys, span_values, cited_spans, cite_count, out_weight):
    row_count = query_heads.shape[0]
    head_groups = query_heads.shape[1]
    group_heads = query_heads.shape[2]
    head_size = query_heads.shape[3]
    stores = lax.axis_size("store")
    per_shard = span_keys.shape[0]
    span_tokens = span_keys.shape[2]
    per_owner = POOL // stores
    score_scale = head_size ** (-0.5)
    slot_index = jnp.arange(cited_spans.shape[1], dtype=jnp.int32)
    slot_live = slot_index[None, :] < cite_count[:, None]
    every_span = jnp.arange(per_shard * stores, dtype=jnp.int32)
    row_hits = jnp.any(
        (cited_spans[:, :, None] == every_span[None, None, :]) & slot_live[:, :, None], axis=1
    )
    row_cites = row_hits.reshape(row_count, stores, per_shard)
    present = jnp.any(row_cites, axis=0)
    rank_in_shard = jnp.cumsum(present.astype(jnp.int32), axis=1) - 1
    owner_slot = jnp.arange(per_owner, dtype=jnp.int32)
    picked = present[:, None, :] & (rank_in_shard[:, None, :] == owner_slot[None, :, None])
    local_index = jnp.arange(per_shard, dtype=jnp.int32)
    needed = jnp.sum(jnp.where(picked, local_index[None, None, :], 0), axis=-1)
    pool_flags = jnp.any(row_cites[:, :, None, :] & picked[None], axis=-1)
    wanted = lax.all_to_all(needed, "store", split_axis=0, concat_axis=0, tiled=True)
    wanted_flat = wanted.reshape(-1)
    send_keys = span_keys[wanted_flat].reshape(
        stores, per_owner, head_groups, span_tokens, head_size
    )
    send_values = span_values[wanted_flat].reshape(
        stores, per_owner, head_groups, span_tokens, head_size
    )
    got_keys, got_values = (
        lax.all_to_all(send_keys, "store", split_axis=0, concat_axis=0, tiled=True),
        lax.all_to_all(send_values, "store", split_axis=0, concat_axis=0, tiled=True),
    )
    pool_keys = got_keys.reshape(stores * per_owner, head_groups, span_tokens, head_size)
    pool_values = got_values.reshape(stores * per_owner, head_groups, span_tokens, head_size)
    scores = (
        jnp.einsum("rkgd,pktd->rkgpt", query_heads, pool_keys, preferred_element_type=jnp.float32)
        * score_scale
    )
    span_top = jnp.max(scores, axis=-1)
    probs = jnp.exp(scores - span_top[..., None])
    probs_low = probs.astype(jnp.bfloat16)
    span_sum = jnp.sum(probs, axis=-1)
    span_out = jnp.einsum(
        "rkgpt,pktd->rkgpd", probs_low, pool_values, preferred_element_type=jnp.float32
    )
    pool_mask = pool_flags.reshape(row_count, 1, 1, stores * per_owner)
    row_top = jnp.max(jnp.where(pool_mask, span_top, -1e30), axis=-1)
    weights = jnp.where(pool_mask, jnp.exp(span_top - row_top[..., None]), 0.0)
    numer = jnp.sum(weights[..., None] * span_out, axis=3)
    denom = jnp.sum(weights * span_sum, axis=-1)
    attn = (numer / denom[..., None]).astype(jnp.bfloat16)
    flat_attn = attn.reshape(row_count, head_groups * group_heads * head_size)
    projected = jnp.dot(
        lax.all_gather(flat_attn, "store", axis=0, tiled=True),
        out_weight,
        preferred_element_type=jnp.float32,
    )
    return lax.psum_scatter(projected, "kvh", scatter_dimension=0, tiled=True).astype(jnp.bfloat16)


def solution(mesh):
    return jax.shard_map(
        per_device,
        mesh=mesh,
        in_specs=(
            P("store", "kvh", None, None),
            P("store", "kvh", None, None),
            P("store", "kvh", None, None),
            P("store", None),
            P("store"),
            P("kvh", "store"),
        ),
        out_specs=P("kvh", "store"),
        check_vma=False,
    )
```

profile of v0, /device:TPU:6, one launch (start us, length us, event | category | flops | bytes accessed | tf_op | source)
XLA Modules:
  0.0 571.6 jit_solution(9547824377132792994)
XLA Ops:
  6.5 0.9 iota_compare_fusion.2
  7.4 1.4 fusion.13
  9.0 0.2 reduce_window_sum.11
  9.3 21.1 %all_to_all.19 = s32[32,1,2]{2,1,0:T(1,128)S(1)} all-to-all(s32[32,1,2]{2,1,0:T(1,128)S(1)} %copy.24), channel_id=1, replica_groups=mesh['kvh'=8,'store'=32] {'store'}, dimensions={0} | all-to-all | bytes 512 | tf_op jit(solution)/shard_map/all_to_all | solution.py:33
  30.4 0.5 broadcast.121
  30.9 0.7 reduce.12
  31.8 5.2 gather_fusion
  37.0 5.1 all-to-all-start.1
  42.1 5.2 gather_fusion.1
  47.3 180.2 %all-to-all-done.1 = bf16[32,2,1,512,128]{4,3,1,2,0:T(8,128)(2,1)} async-done(((bf16[32,2,1,512,128]{4,3,1,2,0:T(8,128)(2,1)}), bf16[32,2,1,512,128]{4,3,1,2,0:T(8,128)(2,1)}, u32[]{:S(2)}, u32[]{:S(2)}) %all-to-all-start.1) | async-done | bytes 8388640 | tf_op jit(solution)/shard_map/all_to_all | solution.py:42
  227.5 10.2 %all-to-all-start.2 = ((bf16[32,2,1,512,128]{4,3,1,2,0:T(8,128)(2,1)}), bf16[32,2,1,512,128]{4,3,1,2,0:T(8,128)(2,1)}, u32[]{:S(2)}, u32[]{:S(2)}) async-start(bf16[32,2,1,512,128]{4,3,1,2,0:T(8,128)(2,1)} %bitcast.64), calls=%async_computation.2 | async-start | bytes 16777216 | tf_op jit(solution)/shard_map/all_to_all | solution.py:43
  237.7 0.2 copy.19
  237.9 0.2 copy.20
  238.1 0.2 and_reduce_fusion
  238.3 0.1 copy.23
  238.5 16.6 %bitcast_reduce_fusion = (f32[32,8,64]{0,1,2:T(8,128)S(1)}, f32[64,512,32,8]{1,2,3,0:T(8,128)}) fusion(bf16[64,512,128,1]{2,1,3,0:T(8,128)(2,1)} %bitcast.7, bf16[32,8,128]{2,1,0:T(8,128)(2,1)S(1)} %bitcast.67), kind=kOutput, calls=%fused_computation.3 | convolution fusion | flops 2164244480 | bytes 42074112 | tf_op jit(solution)/shard_map/rkgd,pktd->rkgpt/dot_general | solution.py:48
  255.1 14.8 %fusion.1 = f32[32,8,64]{0,1,2:T(8,128)S(1)} fusion(f32[64,512,32,8]{1,2,3,0:T(8,128)} %get-tuple-element.12, f32[32,8,64]{0,1,2:T(8,128)S(1)} %get-tuple-element.11), kind=kLoop, calls=%fused_computation.5 | loop fusion | flops 25149440 | bytes 33685504 | tf_op jit(solution)/shard_map/reduce_sum | solution.py:54
  270.0 157.1 %all-to-all-done.2 = bf16[32,2,1,512,128]{4,3,1,2,0:T(8,128)(2,1)} async-done(((bf16[32,2,1,512,128]{4,3,1,2,0:T(8,128)(2,1)}), bf16[32,2,1,512,128]{4,3,1,2,0:T(8,128)(2,1)}, u32[]{:S(2)}, u32[]{:S(2)}) %all-to-all-start.2) | async-done | bytes 8388640 | tf_op jit(solution)/shard_map/all_to_all | solution.py:43
  427.1 16.8 %fusion.8 = f32[32,8,128]{2,0,1:T(8,128)S(1)} fusion(f32[32,8,64]{0,1,2:T(8,128)S(1)} %get-tuple-element.8, bf16[64,512,128,1]{2,1,3,0:T(8,128)(2,1)} %bitcast.16, f32[64,512,32,8]{1,2,3,0:T(8,128)} %get-tuple-element.12, f32[32,8,64]{0,1,2:T(8,128)S(1)} %get-tuple-element.11), kind=kOutput, calls=%fused_computation.12 | convolution fusion | flops 2176811008 | bytes 42205184 | tf_op jit(solution)/shard_map/rkgpt,pktd->rkgpd/dot_general | solution.py:55
  444.0 0.7 copy_bitcast_fusion
  444.8 86.4 %all-gather.2.cloned.1.call-done = bf16[1024,1024]{1,0:T(8,128)(2,1)} async-done(((bf16[32,1024]{1,0:T(8,128)(2,1)}), bf16[1024,1024]{1,0:T(8,128)(2,1)}) %all-gather.2.cloned.1.call-update) | async-done | bytes 2097168 | tf_op jit(solution)/shard_map/all_gather | solution.py:66
  531.2 3.3 fusion.22
  534.5 28.7 %reduce-scatter.2.cloned.1.call-done = f32[128,256]{1,0:T(8,128)} async-done(((f32[1024,256]{1,0:T(8,128)}), f32[128,256]{1,0:T(8,128)}) %reduce-scatter.2.cloned.1.call-update) | async-done | bytes 131088 | tf_op jit(solution)/shard_map/reduce_scatter | solution.py:70
  563.2 1.5 convert_element_type.26
  (27 shorter events, 0.8 us)
Async XLA Ops:
  6.5 25.2 %copy-start = (bf16[16,1,512,128]{3,2,1,0:T(8,128)(2,1)S(1)}, bf16[16,1,512,128]{3,2,1,0:T(8,128)(2,1)}, u32[]{:S(2)}) copy-start(bf16[16,1,512,128]{3,2,1,0:T(8,128)(2,1)} %param.7) | copy-start | bytes 6291460
  37.0 5.1 copy-start.2
  37.0 190.5 %all-to-all-start.1 = ((bf16[32,2,1,512,128]{4,3,1,2,0:T(8,128)(2,1)}), bf16[32,2,1,512,128]{4,3,1,2,0:T(8,128)(2,1)}, u32[]{:S(2)}, u32[]{:S(2)}) async-start(bf16[32,2,1,512,128]{4,3,1,2,0:T(8,128)(2,1)} %bitcast.65), calls=%async_computation.1 | async-start | bytes 16777216 | tf_op jit(solution)/shard_map/all_to_all | solution.py:42
  227.5 11.0 %copy-start.3 = (bf16[32,1,8,128]{3,2,1,0:T(8,128)(2,1)S(1)}, bf16[32,1,8,128]{3,2,1,0:T(8,128)(2,1)}, u32[]{:S(2)}) copy-start(bf16[32,1,8,128]{3,2,1,0:T(8,128)(2,1)} %param.6) | copy-start | bytes 196612
  227.5 199.7 %all-to-all-start.2 = ((bf16[32,2,1,512,128]{4,3,1,2,0:T(8,128)(2,1)}), bf16[32,2,1,512,128]{4,3,1,2,0:T(8,128)(2,1)}, u32[]{:S(2)}, u32[]{:S(2)}) async-start(bf16[32,2,1,512,128]{4,3,1,2,0:T(8,128)(2,1)} %bitcast.64), calls=%async_computation.2 | async-start | bytes 16777216 | tf_op jit(solution)/shard_map/all_to_all | solution.py:43
  237.7 293.5 %all-gather.2.cloned.1.call-start = ((), (), s32[]{:S(2)}) async-start(), calls=%async_computation.4 | async-start | bytes 2162688 | tf_op jit(solution)/shard_map/all_gather | solution.py:66
  427.1 104.1 %copy-start.4 = (bf16[1024,256]{1,0:T(8,128)(2,1)S(1)}, bf16[1024,256]{1,0:T(8,128)(2,1)}, u32[]{:S(2)}) copy-start(bf16[1024,256]{1,0:T(8,128)(2,1)} %param.11) | copy-start | bytes 1572868
  427.1 137.6 %copy-start.1 = (bf16[16,1,512,128]{3,2,1,0:T(8,128)(2,1)S(1)}, bf16[16,1,512,128]{3,2,1,0:T(8,128)(2,1)}, u32[]{:S(2)}) copy-start(bf16[16,1,512,128]{3,2,1,0:T(8,128)(2,1)} %param.7) | copy-start | bytes 6291460
  444.7 118.5 %reduce-scatter.2.cloned.1.call-start = ((), (), s32[]{:S(2)}) async-start(), calls=%async_computation.5 | async-start | bytes 1179648 | tf_op jit(solution)/shard_map/reduce_scatter | solution.py:70
Sparse Core Ops, SparseCore 0:
  444.8 86.3 all-gather.1
  534.6 28.5 reduce-scatter.1
where the time goes:
time: 575 us; the launch traced here: 572 us
  waiting for transfers between devices  452 us (79%)
  matrix products  36.7 us (6%)
  blocking collectives  21.1 us (4%)
  other arithmetic  20.5 us (4%)
  starting transfers between devices  15.4 us (3%)
  between operations  13.5 us (2%)
  local copies, waits for them, and re-layouts  11.9 us (2%)
    all_to_all x1, waiting for transfers between devices, per_device(): lax.all_to_all(send_keys, 'store', split_axis=0, concat_axis=0, tiled=True)  180 us
    all_to_all x1, waiting for transfers between devices, per_device(): lax.all_to_all(send_values, 'store', split_axis=0, concat_axis=0, tiled=T...  157 us
    all_gather x1, waiting for transfers between devices, per_device(): lax.all_gather(flat_attn, 'store', axis=0, tiled=True)  86.4 us
    reduce_scatter x1, waiting for transfers between devices, per_device(): lax.psum_scatter(projected, 'kvh', scatter_dimension=0, tiled=True)  28.7 us
    all_to_all x1, blocking collectives, per_device(): lax.all_to_all(needed, 'store', split_axis=0, concat_axis=0, tiled=True)  21.1 us
    dot_general x1, matrix products, per_device(): jnp.einsum('rkgpt,pktd->rkgpd', probs_low, pool_values, preferred_element...  16.8 us
    dot_general x1, matrix products, per_device(): jnp.einsum('rkgd,pktd->rkgpt', query_heads, pool_keys, preferred_element_...  16.6 us
    reduce_sum x1, other arithmetic, per_device(): span_sum = jnp.sum(probs, axis=-1)  14.8 us
  transfers between devices with their start and end apart: 4, of which 4 were waited for; matrix products, arithmetic and copies ran while one was open for 7% of the time, Pallas kernels for 0%

commit v1 on v0

v1 whole, which is shorter than its diff:
```python
import functools
import math

import jax
import jax.numpy as jnp
from jax import lax
from jax.experimental import pallas as pl
from jax.experimental.pallas import tpu as pltpu
from jax.sharding import Mesh, PartitionSpec as P

HEADS = 8
HEAD = 128
FLAT = HEADS * HEAD
WIDE = FLAT + 128
NEG = -1e30
BIG = 1e30
EXP_SCALE = HEAD**-0.5 * math.log2(math.e)
F32 = jnp.float32
BF16 = jnp.bfloat16
SUM_SENT = BF16
VMEM_LIMIT = 28 * 1024 * 1024


def shift(x, axis, size, step):
    return lax.ppermute(x, axis, [(i, (i + step) % size) for i in range(size)])


def lane_ids(rows):
    return lax.broadcasted_iota(jnp.int32, (rows, 128), 1)


def pack_stats(stats):
    lane = lane_ids(stats.shape[0])
    spread = jnp.where(
        (lane // 8) % 3 == 0,
        stats,
        jnp.where((lane // 8) % 3 == 1, pltpu.roll(stats, 8, 1), pltpu.roll(stats, 16, 1)),
    )
    high = spread.astype(BF16).astype(F32)
    rest = spread - high
    middle = rest.astype(BF16).astype(F32)
    low = rest - middle
    terms = jnp.where(
        (lane // 8) % 3 == 0, high, jnp.where((lane // 8) % 3 == 1, middle, low)
    )
    return jnp.where(lane < 48, terms, 0.0).astype(BF16)


def unpack_stats(packed):
    terms = packed.astype(F32)
    return terms + (pltpu.roll(terms, 120, 1) + pltpu.roll(terms, 112, 1))


def find_spans(me, q):
    code = q[:, FLAT:].astype(F32)
    span = jnp.where(code > 0, code - 1.0, 255.0 - code) - 16.0 * me
    mine = (code != 0) & (span >= 0) & (span < 16)
    first = jnp.min(jnp.where(mine, span, 99.0))
    second = jnp.max(jnp.where(mine, span, -1.0))
    picks = []
    for chosen in (first, second):
        live = jnp.max(jnp.where(mine & (span == chosen), 1.0, 0.0), axis=1, keepdims=True)
        at = jnp.clip(chosen.astype(jnp.int32), 0, 15)
        picks.append((at, jnp.concatenate([live] * HEADS, axis=0) > 0))
    return picks


def score(q, picks, k_ref):
    queries = jnp.concatenate([q[:, h * HEAD : (h + 1) * HEAD] for h in range(HEADS)], axis=0)
    return [
        lax.dot_general(queries, k_ref[at], (((1,), (1,)), ((), ())), preferred_element_type=F32)
        for at, _ in picks
    ]


def weigh(scores, picks, v_ref):
    top = None
    for s, (_, live) in zip(scores, picks):
        lanes = [s[:, i : i + 128] for i in range(0, s.shape[1], 128)]
        part = jnp.where(live, functools.reduce(jnp.maximum, lanes), NEG)
        top = part if top is None else jnp.maximum(top, part)
    top = jnp.max(top, axis=1, keepdims=True)
    both = None
    for s, (at, live) in zip(scores, picks):
        probs = jnp.exp2((s - jnp.where(live, top, BIG)) * EXP_SCALE).astype(BF16)
        span = v_ref[at]
        ones = jnp.concatenate([span, jnp.ones_like(span)], axis=1)
        out = jnp.dot(probs, ones, preferred_element_type=F32)
        both = out if both is None else both + out
    rows = top.shape[0] // HEADS
    lane = lane_ids(rows)
    stats = jnp.zeros((rows, 128), F32)
    heads = []
    for h in range(HEADS):
        part = slice(h * rows, (h + 1) * rows)
        denom = both[part, HEAD : HEAD + 1]
        stats = jnp.where(lane == h, top[part], jnp.where(lane == 24 + h, denom, stats))
        heads.append(both[part, :HEAD])
    return heads, stats


def put_packed(out_ref, at, heads, stats):
    for h, numer in enumerate(heads):
        out_ref[at, :, h * HEAD : (h + 1) * HEAD] = numer.astype(BF16)
    out_ref[at, :, FLAT:] = pack_stats(stats)


def attend_kernel(layout, before, me_ref, *refs):
    count = 1 + max(ref for ref, _, _, _ in layout)
    q_refs, (k_ref, v_ref), refs = refs[:count], refs[count : count + 2], refs[count + 2 :]
    outs = refs[-4:]
    for out, done in zip(outs, refs[:-4]):
        out[:before] = done[...]
    me = me_ref[0].astype(F32)
    picks = [find_spans(me, q_refs[ref][at]) for ref, at, _, _ in layout]
    ahead = score(q_refs[layout[0][0]][layout[0][1]], picks[0], k_ref)
    for i, (_, _, b, g) in enumerate(layout):
        scores = ahead
        if i + 1 < len(layout):
            ref, at, _, _ = layout[i + 1]
            ahead = score(q_refs[ref][at], picks[i + 1], k_ref)
        heads, stats = weigh(scores, picks[i], v_ref)
        if g:
            put_packed(outs[g], before + b, heads, stats)
            continue
        for h, numer in enumerate(heads):
            outs[0][before + b, :, h * HEAD : (h + 1) * HEAD] = numer
        outs[0][before + b, :, FLAT:] = stats


def local_call(kernel, name, scalars, inputs, out_shape, flops=0, exps=0):
    vmem = pl.BlockSpec(memory_space=pltpu.VMEM)
    size = sum(i.size * i.dtype.itemsize for i in list(inputs) + list(out_shape))
    return pl.pallas_call(
        kernel,
        out_shape=out_shape,
        in_specs=[pl.BlockSpec(memory_space=pltpu.SMEM)] * len(scalars) + [vmem] * len(inputs),
        out_specs=[vmem] * len(out_shape),
        compiler_params=pltpu.CompilerParams(vmem_limit_bytes=VMEM_LIMIT),
        cost_estimate=pl.CostEstimate(flops=flops, bytes_accessed=size, transcendentals=exps),
        name=name,
    )(*scalars, *inputs)


def attend(me, parts, keys, values, done=()):
    layout, place = [], 0
    for ref, part in enumerate(parts):
        for at in range(part.shape[0]):
            layout.append((ref, at, place // 4, place % 4))
            place += 1
    rows, before = parts[0].shape[1], done[0].shape[0] if done else 0
    out = [
        jax.ShapeDtypeStruct((before + place // 4, rows, WIDE), t) for t in (F32, BF16, BF16, BF16)
    ]
    work = place * 256 * 1024
    return local_call(
        functools.partial(attend_kernel, layout, before),
        "attend",
        [me],
        [*parts, keys, values, *done],
        out,
        flops=work * 4 * HEAD,
        exps=work,
    )


def packed_part(ref, at):
    return ref[at, :, :FLAT], unpack_stats(ref[at, :, FLAT:])


def join(parts):
    top = functools.reduce(jnp.maximum, [s for _, s in parts])
    weights = [jnp.exp2((s - top) * EXP_SCALE) for _, s in parts]
    denom = functools.reduce(
        jnp.add, [pltpu.roll(w, 24, 1) * s for w, (_, s) in zip(weights, parts)]
    )
    heads = []
    for h in range(HEADS):
        lanes = slice(h * HEAD, (h + 1) * HEAD)
        heads.append(
            functools.reduce(
                jnp.add,
                [w[:, h : h + 1] * n[:, lanes].astype(F32) for w, (n, _) in zip(weights, parts)],
            )
        )
    return heads, top, denom


def line_kernel(batches, first, z_ref, *refs):
    out_ref, mine_ref = refs[-2:]
    z = z_ref[0]
    if first:
        out_ref[...], mine_ref[...] = refs[-4][...], refs[-3][...]
    place = first
    for batch, size in enumerate(batches):
        own_ref, got = refs[4 * batch], refs[4 * batch + 1 : 4 * batch + 4]
        for b in range(size):
            step, place = STEPS[place], place + 1
            parts = [(own_ref[b, :, :FLAT], own_ref[b, :, FLAT:])]
            heads, top, denom = join(parts + [packed_part(r, b) for r in got])
            stats = jnp.where(lane_ids(top.shape[0]) < 24, top, denom)
            put_packed(out_ref, lax.rem(z + step + 8, 8), heads, stats)
            if step == 0:
                for h, numer in enumerate(heads):
                    mine_ref[:, h * HEAD : (h + 1) * HEAD] = numer
                mine_ref[:, FLAT:] = stats


def finish_kernel(z_ref, mine_ref, got_ref, out_ref):
    z = z_ref[0]
    parts = [(mine_ref[:, :FLAT], mine_ref[:, FLAT:])]
    parts += [packed_part(got_ref, lax.rem(z + step, 8)) for step in range(1, 8)]
    heads, _, denom = join(parts)
    for h, numer in enumerate(heads):
        attn = (numer / denom[:, 24 + h : 25 + h]).astype(BF16)
        for copy in range(8):
            out_ref[copy, :, h * HEAD : (h + 1) * HEAD] = attn


def project_kernel(core_ref, turn_ref, attn_ref, *refs):
    w_refs, (keep_ref, give_ref) = refs[:4], refs[4:]
    core = core_ref[0]
    for out_ref, half in ((give_ref, 1 - core), (keep_ref, core)):
        rows = attn_ref[pl.ds(half * 4, 4)].reshape(-1, FLAT)
        for back, w_ref in enumerate(w_refs):
            out_ref[lax.rem(turn_ref[0] - back + 8, 4)] = jnp.dot(
                rows, w_ref[...], preferred_element_type=F32
            )


STEPS = (0, -1, 1, -2, 2, -3, 3, 4)


def per_device(query_heads, span_keys, span_values, cited_spans, cite_count, out_weight):
    rows, columns = query_heads.shape[0], out_weight.shape[1]
    x, core, y, z = (lax.axis_index(a).astype(jnp.int32) for a in ("x", "core", "y", "z"))
    me, my_z = (y * 8 + z).reshape(1), z.reshape(1)
    slot = jnp.arange(cited_spans.shape[1], dtype=jnp.int32)
    code = jnp.where(cited_spans < 256, cited_spans + 1, 255 - cited_spans)
    code = jnp.where(slot[None, :] < cite_count[:, None], code, 0).astype(BF16)
    wide = jnp.concatenate(
        [query_heads.reshape(rows, FLAT), code, jnp.zeros((rows, 128 - code.shape[1]), BF16)], axis=1
    )
    keys, values = span_keys[:, 0], span_values[:, 0]

    def send(parts):
        return [parts[0]] + [shift(o, "y", 4, -s) for s, o in zip((1, 2, 3), parts[1:])]

    tie = lax.optimization_barrier
    own = jnp.stack([wide] + [shift(wide, "y", 4, step) for step in (1, 2, 3)])
    low_1, high_1 = shift(own, "z", 8, 1), shift(own, "z", 8, -1)
    near = attend(me, [own], keys, values)
    low_1, high_1, near = tie((low_1, high_1, near))
    low_2, high_2 = shift(low_1, "z", 8, 1), shift(high_1, "z", 8, -1)
    near = attend(me, [low_1, high_1], keys, values, near)
    weights = [shift(out_weight, "y", 4, step) for step in (1, 3)]
    low_2, high_2, near = tie((low_2, high_2, near))
    low_3, high_3 = shift(low_2, "z", 8, 1), shift(high_2, "z", 8, -1)
    near = attend(me, [low_2, high_2], keys, values, near)
    low_3, high_3, near, weights, out_weight = tie((low_3, high_3, near, weights, out_weight))
    far = [shift(low_3[:2], "z", 8, 1), shift(high_3[2:], "z", 8, -1)]
    near = send(near)
    beyond = attend(me, [low_3, high_3], keys, values)
    far, beyond, out_weight = tie((far, beyond, out_weight))
    beyond = send(attend(me, far, keys, values, beyond))
    weights = [out_weight, weights[0], shift(out_weight, "y", 4, 2), weights[1]]

    line = [jax.ShapeDtypeStruct((8, rows, WIDE), BF16), jax.ShapeDtypeStruct((rows, WIDE), F32)]
    joined = local_call(functools.partial(line_kernel, [5], 0), "line", [my_z], near, line)
    joined, mine = local_call(
        functools.partial(line_kernel, [3], 5), "line", [my_z], [*beyond, *joined], line
    )
    got = lax.all_to_all(joined, "z", 0, 0, tiled=True)
    got, weights = tie((got, weights))
    (attn,) = local_call(
        finish_kernel, "finish", [my_z], [mine, got], [jax.ShapeDtypeStruct((8, rows, FLAT), BF16)]
    )
    attn = lax.all_to_all(attn, "z", 0, 0, tiled=True)

    half = jax.ShapeDtypeStruct((4, 4 * rows, columns), F32)
    keep, give = local_call(
        project_kernel,
        "project",
        [core.reshape(1), (y - x).reshape(1)],
        [attn, *weights],
        [half, half],
        flops=2 * 1024 * FLAT * columns,
    )
    sums = keep + shift(give, "core", 2, 1)
    total = sums[0]
    for step in (1, 2, 3):
        total = total + shift(sums[step].astype(SUM_SENT), "x", 4, step).astype(F32)
    swap = [(a * 4 + b, b * 4 + a) for a in range(4) for b in range(4)]
    return lax.ppermute(total.astype(BF16), ("x", "y"), swap)


def solution(mesh):
    split = Mesh(mesh.devices.reshape(4, 2, 4, 8), ("x", "core", "y", "z"))
    heads, store = ("x", "core"), ("y", "z")
    return jax.shard_map(
        per_device,
        mesh=split,
        in_specs=(
            P(store, heads, None, None),
            P(store, heads, None, None),
            P(store, heads, None, None),
            P(store, None),
            P(store),
            P(heads, store),
        ),
        out_specs=P(heads, store),
        check_vma=False,
    )
```

time: 575 us -> 132 us (0.23)
  waiting for transfers between devices: 452 us -> 56.4 us
  matrix products: 36.7 us -> 0 us
  starting transfers between devices: 15.4 us -> 48.8 us
  blocking collectives: 21.1 us -> 0 us
  Pallas kernels: 0 us -> 20.8 us
  other arithmetic: 20.5 us -> 0.98 us
  between operations: 13.5 us -> 0.17 us
  local copies, waits for them, and re-layouts: 11.9 us -> 4.81 us
    all_to_all x2, waiting for transfers between devices: 337 us -> 16.8 us  [the longest x1 13.3 us: per_device(): attn = lax.all_to_all(attn, 'z', 0, 0, tiled=True)]
    all_gather x1 -> x0, waiting for transfers between devices: 86.4 us -> none  [per_device(): lax.all_gather(flat_attn, 'store', axis=0, tiled=True)]
    ppermute x0 -> x25, starting transfers between devices: none -> 39.6 us  [the longest x24 36.7 us: shift(): return lax.ppermute(x, axis, [(i, (i + step) % size) for i in range(size)])]
    ppermute x0 -> x25, waiting for transfers between devices: none -> 39.6 us  [the longest x24 33.1 us: shift(): return lax.ppermute(x, axis, [(i, (i + step) % size) for i in range(size)])]
    dot_general x3 -> x0, matrix products: 36.7 us -> none  [the longest x1 16.8 us: per_device(): jnp.einsum('rkgpt,pktd->rkgpd', probs_low, pool_values, preferred_element...]
    reduce_scatter x1 -> x0, waiting for transfers between devices: 28.7 us -> none  [per_device(): lax.psum_scatter(projected, 'kvh', scatter_dimension=0, tiled=True)]
    all_to_all x1 -> x0, blocking collectives: 21.1 us -> none  [per_device(): lax.all_to_all(needed, 'store', split_axis=0, concat_axis=0, tiled=True)]
    pallas_call x0 -> x9, Pallas kernels: none -> 20.8 us  [local_call(): pl.pallas_call(kernel, out_shape=out_shape, in_specs=[pl.BlockSpec(memory...]
  transfers between devices with their start and end apart: 4 -> 27, of which waited for: 4 -> 16; matrix products, arithmetic and copies ran while one was open for 7% -> 0% of each run, Pallas kernels for 0% -> 13%
where the time goes in v1:
time: 132 us
  waiting for transfers between devices  56.4 us (43%)
  starting transfers between devices  48.8 us (37%)
  Pallas kernels  20.8 us (16%)
  local copies, waits for them, and re-layouts  4.81 us (4%)
    ppermute x24, starting transfers between devices, shift(): return lax.ppermute(x, axis, [(i, (i + step) % size) for i in range(size)])  36.7 us
    ppermute x24, waiting for transfers between devices, shift(): return lax.ppermute(x, axis, [(i, (i + step) % size) for i in range(size)])  33.1 us
    pallas_call x9, Pallas kernels, local_call(): pl.pallas_call(kernel, out_shape=out_shape, in_specs=[pl.BlockSpec(memory...  20.8 us
    all_to_all x1, waiting for transfers between devices, per_device(): attn = lax.all_to_all(attn, 'z', 0, 0, tiled=True)  13.3 us
    ppermute x1, waiting for transfers between devices, per_device(): return lax.ppermute(total.astype(BF16), ('x', 'y'), swap)  6.54 us
    all_to_all x1, starting transfers between devices, per_device(): got = lax.all_to_all(joined, 'z', 0, 0, tiled=True)  5.48 us
    unnamed x10, local copies, waits for them, and re-layouts  4.67 us
    all_to_all x1, starting transfers between devices, per_device(): attn = lax.all_to_all(attn, 'z', 0, 0, tiled=True)  3.68 us
  transfers between devices with their start and end apart: 27, of which 16 were waited for; matrix products, arithmetic and copies ran while one was open for 0% of the time, Pallas kernels for 13%

profile of v1, /device:TPU:6, one launch (start us, length us, event | category | flops | bytes accessed | tf_op | source)
XLA Modules:
  0.0 132.0 jit_solution(13299468968509292136)
XLA Ops:
  3.4 2.9 %collective-permute-start.1 = (bf16[32,1152]{1,0:T(8,128)(2,1)S(1)}, bf16[32,1152]{1,0:T(8,128)(2,1)S(1)}, u32[]{:S(2)}, u32[]{:S(2)}) collective-permute-start(bf16[32,1152]{1,0:T(8,128)(2,1)S(1)} %concatenate.3), channel_id=1, source_target_pairs={{0,16},{8,24},{16,0},{24,8},{1,17},{9,25},{17,1},{25,9},{2,18},{10... | collective-permute-start | bytes 221192 | tf_op jit(solution)/shard_map/ppermute | solution.py:25
  7.6 2.2 %collective-permute-done.1 = bf16[32,1152]{1,0:T(8,128)(2,1)S(1)} collective-permute-done((bf16[32,1152]{1,0:T(8,128)(2,1)S(1)}, bf16[32,1152]{1,0:T(8,128)(2,1)S(1)}, u32[]{:S(2)}, u32[]{:S(2)}) %collective-permute-start.1) | collective-permute-done | bytes 73760 | tf_op jit(solution)/shard_map/ppermute | solution.py:25
  12.7 4.0 %collective-permute-start.4 = (bf16[4,32,1152]{2,1,0:T(8,128)(2,1)S(1)}, bf16[4,32,1152]{2,1,0:T(8,128)(2,1)S(1)}, u32[]{:S(2)}, u32[]{:S(2)}) collective-permute-start(bf16[4,32,1152]{2,1,0:T(8,128)(2,1)S(1)} %pad_maximum_fusion.refs_0_), channel_id=1, source_target_pairs={{0,7},{1,0},{2,1},{3,2},{4,3},{5,4},{6,5},{7,6},{8,15},{9,8},{10,9... | collective-permute-start | bytes 884744 | tf_op jit(solution)/shard_map/ppermute | solution.py:25
  22.3 3.2 %collective-permute-start.6 = (bf16[4,32,1152]{2,1,0:T(8,128)(2,1)S(1)}, bf16[4,32,1152]{2,1,0:T(8,128)(2,1)S(1)}, u32[]{:S(2)}, u32[]{:S(2)}) collective-permute-start(bf16[4,32,1152]{2,1,0:T(8,128)(2,1)S(1)} %collective-permute-done.4.refs_1_), channel_id=1, source_target_pairs={{0,7},{1,0},{2,1},{3,2},{4,3},{5,4},{6,5},{7,6},{8,15},{9,8},{10,9... | collective-permute-start | bytes 884744 | tf_op jit(solution)/shard_map/ppermute | solution.py:25
  25.5 2.4 %collective-permute-start.10 = (bf16[1024,256]{1,0:T(8,128)(2,1)S(1)}, bf16[1024,256]{1,0:T(8,128)(2,1)S(1)}, u32[]{:S(2)}, u32[]{:S(2)}) collective-permute-start(bf16[1024,256]{1,0:T(8,128)(2,1)S(1)} %copy-done.3), channel_id=1, source_target_pairs={{0,24},{8,0},{16,8},{24,16},{1,25},{9,1},{17,9},{25,17},{2,26},{10... | collective-permute-start | bytes 1572872 | tf_op jit(solution)/shard_map/ppermute | solution.py:25
  27.9 3.5 %attend.6 = (f32[3,32,1152]{2,1,0:T(8,128)S(1)}, bf16[3,32,1152]{2,1,0:T(8,128)(2,1)S(1)}, bf16[3,32,1152]{2,1,0:T(8,128)(2,1)S(1)}, bf16[3,32,1152]{2,1,0:T(8,128)(2,1)S(1)}) custom-call(s32[1]{0:T(128)} %bitcast.3.me_ref, bf16[4,32,1152]{2,1,0:T(8,128)(2,1)S(1)} %collective-permute-done.3.refs_0_, bf16[4,32,1152]{2,1,0:T(8,128)(2,1)S(1)} %collective-permute-done.4.refs_1_, ...), custom_call_target="tpu_custom_call" | custom-call | flops 1073741824 | bytes 6258688 | tf_op jit(solution)/shard_map/attend/pallas_call | solution.py:134
  32.7 2.2 %collective-permute-start.8 = (bf16[4,32,1152]{2,1,0:T(8,128)(2,1)S(1)}, bf16[4,32,1152]{2,1,0:T(8,128)(2,1)S(1)}, u32[]{:S(2)}, u32[]{:S(2)}) collective-permute-start(bf16[4,32,1152]{2,1,0:T(8,128)(2,1)S(1)} %collective-permute-done.6.refs_1_), channel_id=1, source_target_pairs={{0,7},{1,0},{2,1},{3,2},{4,3},{5,4},{6,5},{7,6},{8,15},{9,8},{10,9... | collective-permute-start | bytes 884744 | tf_op jit(solution)/shard_map/ppermute | solution.py:25
  34.9 3.7 %attend.7 = (f32[5,32,1152]{2,1,0:T(8,128)S(1)}, bf16[5,32,1152]{2,1,0:T(8,128)(2,1)S(1)}, bf16[5,32,1152]{2,1,0:T(8,128)(2,1)S(1)}, bf16[5,32,1152]{2,1,0:T(8,128)(2,1)S(1)}) custom-call(s32[1]{0:T(128)} %bitcast.3.me_ref, bf16[4,32,1152]{2,1,0:T(8,128)(2,1)S(1)} %collective-permute-done.5.refs_0_, bf16[4,32,1152]{2,1,0:T(8,128)(2,1)S(1)} %collective-permute-done.6.refs_1_, ...), custom_call_target="tpu_custom_call" | custom-call | flops 1073741824 | bytes 7733248 | tf_op jit(solution)/shard_map/attend/pallas_call | solution.py:134
  40.1 2.8 %collective-permute-start.16 = (bf16[5,32,1152]{2,1,0:T(8,128)(2,1)S(1)}, bf16[5,32,1152]{2,1,0:T(8,128)(2,1)S(1)}, u32[]{:S(2)}, u32[]{:S(2)}) collective-permute-start(bf16[5,32,1152]{2,1,0:T(8,128)(2,1)S(1)} %get-tuple-element.106), channel_id=1, source_target_pairs={{0,24},{8,0},{16,8},{24,16},{1,25},{9,1},{17,9},{25,17},{2,26},{10... | collective-permute-start | bytes 1105928 | tf_op jit(solution)/shard_map/ppermute | solution.py:25
  44.2 2.3 %collective-permute-start.12 = (bf16[2,32,1152]{2,1,0:T(8,128)(2,1)S(1)}, bf16[2,32,1152]{2,1,0:T(8,128)(2,1)S(1)}, u32[]{:S(2)}, u32[]{:S(2)}) collective-permute-start(bf16[2,32,1152]{2,1,0:T(8,128)(2,1)S(1)} %slice.22), channel_id=1, source_target_pairs={{0,7},{1,0},{2,1},{3,2},{4,3},{5,4},{6,5},{7,6},{8,15},{9,8},{10,9... | collective-permute-start | bytes 442376 | tf_op jit(solution)/shard_map/ppermute | solution.py:25
  47.4 3.5 %attend.8 = (f32[2,32,1152]{2,1,0:T(8,128)S(1)}, bf16[2,32,1152]{2,1,0:T(8,128)(2,1)S(1)}, bf16[2,32,1152]{2,1,0:T(8,128)(2,1)S(1)}, bf16[2,32,1152]{2,1,0:T(8,128)(2,1)S(1)}) custom-call(s32[1]{0:T(128)} %bitcast.3.me_ref, bf16[4,32,1152]{2,1,0:T(8,128)(2,1)S(1)} %collective-permute-done.7.refs_0_, bf16[4,32,1152]{2,1,0:T(8,128)(2,1)S(1)} %collective-permute-done.8.refs_1_, ...), custom_call_target="tpu_custom_call" | custom-call | flops 1073741824 | bytes 5521408 | tf_op jit(solution)/shard_map/attend/pallas_call | solution.py:134
  50.9 2.1 %attend.9 = (f32[3,32,1152]{2,1,0:T(8,128)S(1)}, bf16[3,32,1152]{2,1,0:T(8,128)(2,1)S(1)}, bf16[3,32,1152]{2,1,0:T(8,128)(2,1)S(1)}, bf16[3,32,1152]{2,1,0:T(8,128)(2,1)S(1)}) custom-call(s32[1]{0:T(128)} %bitcast.3.me_ref, bf16[2,32,1152]{2,1,0:T(8,128)(2,1)S(1)} %collective-permute-done.11.refs_0_, ...), custom_call_target="tpu_custom_call" | custom-call | flops 536870912 | bytes 6332416 | tf_op jit(solution)/shard_map/attend/pallas_call | solution.py:134
  53.1 2.5 %collective-permute-start.13 = (bf16[3,32,1152]{2,1,0:T(8,128)(2,1)S(1)}, bf16[3,32,1152]{2,1,0:T(8,128)(2,1)S(1)}, u32[]{:S(2)}, u32[]{:S(2)}) collective-permute-start(bf16[3,32,1152]{2,1,0:T(8,128)(2,1)S(1)} %get-tuple-element.102), channel_id=1, source_target_pairs={{0,24},{8,0},{16,8},{24,16},{1,25},{9,1},{17,9},{25,17},{2,26},{10... | collective-permute-start | bytes 663560 | tf_op jit(solution)/shard_map/ppermute | solution.py:25
  55.5 2.3 %collective-permute-start.14 = (bf16[3,32,1152]{2,1,0:T(8,128)(2,1)S(1)}, bf16[3,32,1152]{2,1,0:T(8,128)(2,1)S(1)}, u32[]{:S(2)}, u32[]{:S(2)}) collective-permute-start(bf16[3,32,1152]{2,1,0:T(8,128)(2,1)S(1)} %get-tuple-element.103), channel_id=1, source_target_pairs={{0,16},{8,24},{16,0},{24,8},{1,17},{9,25},{17,1},{25,9},{2,18},{10... | collective-permute-start | bytes 663560 | tf_op jit(solution)/shard_map/ppermute | solution.py:25
  59.7 5.9 %collective-permute-done.18.refs_3_ = bf16[5,32,1152]{2,1,0:T(8,128)(2,1)S(1)} collective-permute-done((bf16[5,32,1152]{2,1,0:T(8,128)(2,1)S(1)}, bf16[5,32,1152]{2,1,0:T(8,128)(2,1)S(1)}, u32[]{:S(2)}, u32[]{:S(2)}) %collective-permute-start.18) | collective-permute-done | bytes 368672 | tf_op jit(solution)/shard_map/ppermute | solution.py:25
  72.5 5.5 %all-to-all-start = ((bf16[8,32,1152]{2,1,0:T(8,128)(2,1)}), bf16[8,32,1152]{2,1,0:T(8,128)(2,1)S(1)}, u32[]{:S(2)}, u32[]{:S(2)}) async-start(bf16[8,32,1152]{2,1,0:T(8,128)(2,1)} %get-tuple-element.112), calls=%async_computation | async-start | bytes 1179648 | tf_op jit(solution)/shard_map/all_to_all | solution.py:273
  78.5 10.1 %collective-permute-done.19.refs_2_ = bf16[1024,256]{1,0:T(8,128)(2,1)S(1)} collective-permute-done((bf16[1024,256]{1,0:T(8,128)(2,1)S(1)}, bf16[1024,256]{1,0:T(8,128)(2,1)S(1)}, u32[]{:S(2)}, u32[]{:S(2)}) %collective-permute-start.19) | collective-permute-done | bytes 524320 | tf_op jit(solution)/shard_map/ppermute | solution.py:25
  88.7 3.5 %all-to-all-done.got_ref = bf16[8,32,1152]{2,1,0:T(8,128)(2,1)S(1)} async-done(((bf16[8,32,1152]{2,1,0:T(8,128)(2,1)}), bf16[8,32,1152]{2,1,0:T(8,128)(2,1)S(1)}, u32[]{:S(2)}, u32[]{:S(2)}) %all-to-all-start) | async-done | bytes 589856 | tf_op jit(solution)/shard_map/all_to_all | solution.py:273
  93.6 3.7 %all-to-all-start.1 = ((bf16[8,32,1024]{2,1,0:T(8,128)(2,1)}), bf16[8,32,1024]{2,1,0:T(8,128)(2,1)S(1)}, u32[]{:S(2)}, u32[]{:S(2)}) async-start(bf16[8,32,1024]{2,1,0:T(8,128)(2,1)} %finish.1), calls=%async_computation.1 | async-start | bytes 1048576 | tf_op jit(solution)/shard_map/all_to_all | solution.py:278
  97.3 13.3 %all-to-all-done.1.attn_ref = bf16[8,32,1024]{2,1,0:T(8,128)(2,1)S(1)} async-done(((bf16[8,32,1024]{2,1,0:T(8,128)(2,1)}), bf16[8,32,1024]{2,1,0:T(8,128)(2,1)S(1)}, u32[]{:S(2)}, u32[]{:S(2)}) %all-to-all-start.1) | async-done | bytes 524320 | tf_op jit(solution)/shard_map/all_to_all | solution.py:278
  113.9 2.4 %collective-permute-start.22 = (bf16[128,256]{1,0:T(8,128)(2,1)S(1)}, bf16[128,256]{1,0:T(8,128)(2,1)S(1)}, u32[]{:S(2)}, u32[]{:S(2)}) collective-permute-start(bf16[128,256]{1,0:T(8,128)(2,1)S(1)} %get-tuple-element.127), channel_id=1, source_target_pairs={{0,128},{64,192},{128,0},{192,64},{1,129},{65,193},{129,1},{193,65... | collective-permute-start | bytes 196616 | tf_op jit(solution)/shard_map/ppermute | solution.py:25
  119.7 2.1 %collective-permute-done.23 = bf16[128,256]{1,0:T(8,128)(2,1)S(1)} collective-permute-done((bf16[128,256]{1,0:T(8,128)(2,1)S(1)}, bf16[128,256]{1,0:T(8,128)(2,1)S(1)}, u32[]{:S(2)}, u32[]{:S(2)}) %collective-permute-start.23) | collective-permute-done | bytes 65568 | tf_op jit(solution)/shard_map/ppermute | solution.py:25
  121.9 2.9 %collective-permute-start.24 = (bf16[128,256]{1,0:T(8,128)(2,1)S(1)}, bf16[128,256]{1,0:T(8,128)(2,1)S(1)}, u32[]{:S(2)}, u32[]{:S(2)}) collective-permute-start(bf16[128,256]{1,0:T(8,128)(2,1)S(1)} %fusion.3), channel_id=1, source_target_pairs={{0,0},{8,64},{16,128},{24,192},{64,8},{72,72},{80,136},{88,200},{1... | collective-permute-start | bytes 196616 | tf_op jit(solution)/shard_map/ppermute | solution.py:294
  124.8 6.5 %collective-permute-done.24 = bf16[128,256]{1,0:T(8,128)(2,1)S(1)} collective-permute-done((bf16[128,256]{1,0:T(8,128)(2,1)S(1)}, bf16[128,256]{1,0:T(8,128)(2,1)S(1)}, u32[]{:S(2)}, u32[]{:S(2)}) %collective-permute-start.24) | collective-permute-done | bytes 65568 | tf_op jit(solution)/shard_map/ppermute | solution.py:294
  (58 shorter events, 36.1 us)
Async XLA Ops:
  1.8 5.9 %collective-permute-start = (bf16[32,1152]{1,0:T(8,128)(2,1)S(1)}, bf16[32,1152]{1,0:T(8,128)(2,1)S(1)}, u32[]{:S(2)}, u32[]{:S(2)}) collective-permute-start(bf16[32,1152]{1,0:T(8,128)(2,1)S(1)} %concatenate.3), channel_id=1, source_target_pairs={{0,8},{8,16},{16,24},{24,0},{1,9},{9,17},{17,25},{25,1},{2,10},{10... | collective-permute-start | bytes 221192 | tf_op jit(solution)/shard_map/ppermute | solution.py:25
  3.4 6.5 %collective-permute-start.1 = (bf16[32,1152]{1,0:T(8,128)(2,1)S(1)}, bf16[32,1152]{1,0:T(8,128)(2,1)S(1)}, u32[]{:S(2)}, u32[]{:S(2)}) collective-permute-start(bf16[32,1152]{1,0:T(8,128)(2,1)S(1)} %concatenate.3), channel_id=1, source_target_pairs={{0,16},{8,24},{16,0},{24,8},{1,17},{9,25},{17,1},{25,9},{2,18},{10... | collective-permute-start | bytes 221192 | tf_op jit(solution)/shard_map/ppermute | solution.py:25
  10.7 11.6 %collective-permute-start.3 = (bf16[4,32,1152]{2,1,0:T(8,128)(2,1)S(1)}, bf16[4,32,1152]{2,1,0:T(8,128)(2,1)S(1)}, u32[]{:S(2)}, u32[]{:S(2)}) collective-permute-start(bf16[4,32,1152]{2,1,0:T(8,128)(2,1)S(1)} %pad_maximum_fusion.refs_0_), channel_id=1, source_target_pairs={{0,1},{1,2},{2,3},{3,4},{4,5},{5,6},{6,7},{7,0},{8,9},{9,10},{10,1... | collective-permute-start | bytes 884744 | tf_op jit(solution)/shard_map/ppermute | solution.py:25
  12.7 9.6 %collective-permute-start.4 = (bf16[4,32,1152]{2,1,0:T(8,128)(2,1)S(1)}, bf16[4,32,1152]{2,1,0:T(8,128)(2,1)S(1)}, u32[]{:S(2)}, u32[]{:S(2)}) collective-permute-start(bf16[4,32,1152]{2,1,0:T(8,128)(2,1)S(1)} %pad_maximum_fusion.refs_0_), channel_id=1, source_target_pairs={{0,7},{1,0},{2,1},{3,2},{4,3},{5,4},{6,5},{7,6},{8,15},{9,8},{10,9... | collective-permute-start | bytes 884744 | tf_op jit(solution)/shard_map/ppermute | solution.py:25
  22.3 9.1 %collective-permute-start.5 = (bf16[4,32,1152]{2,1,0:T(8,128)(2,1)S(1)}, bf16[4,32,1152]{2,1,0:T(8,128)(2,1)S(1)}, u32[]{:S(2)}, u32[]{:S(2)}) collective-permute-start(bf16[4,32,1152]{2,1,0:T(8,128)(2,1)S(1)} %collective-permute-done.3.refs_0_), channel_id=1, source_target_pairs={{0,1},{1,2},{2,3},{3,4},{4,5},{5,6},{6,7},{7,0},{8,9},{9,10},{10,1... | collective-permute-start | bytes 884744 | tf_op jit(solution)/shard_map/ppermute | solution.py:25
  22.3 9.1 %collective-permute-start.6 = (bf16[4,32,1152]{2,1,0:T(8,128)(2,1)S(1)}, bf16[4,32,1152]{2,1,0:T(8,128)(2,1)S(1)}, u32[]{:S(2)}, u32[]{:S(2)}) collective-permute-start(bf16[4,32,1152]{2,1,0:T(8,128)(2,1)S(1)} %collective-permute-done.4.refs_1_), channel_id=1, source_target_pairs={{0,7},{1,0},{2,1},{3,2},{4,3},{5,4},{6,5},{7,6},{8,15},{9,8},{10,9... | collective-permute-start | bytes 884744 | tf_op jit(solution)/shard_map/ppermute | solution.py:25
  25.5 13.1 %collective-permute-start.10 = (bf16[1024,256]{1,0:T(8,128)(2,1)S(1)}, bf16[1024,256]{1,0:T(8,128)(2,1)S(1)}, u32[]{:S(2)}, u32[]{:S(2)}) collective-permute-start(bf16[1024,256]{1,0:T(8,128)(2,1)S(1)} %copy-done.3), channel_id=1, source_target_pairs={{0,24},{8,0},{16,8},{24,16},{1,25},{9,1},{17,9},{25,17},{2,26},{10... | collective-permute-start | bytes 1572872 | tf_op jit(solution)/shard_map/ppermute | solution.py:25
  27.9 12.2 %collective-permute-start.9 = (bf16[1024,256]{1,0:T(8,128)(2,1)S(1)}, bf16[1024,256]{1,0:T(8,128)(2,1)S(1)}, u32[]{:S(2)}, u32[]{:S(2)}) collective-permute-start(bf16[1024,256]{1,0:T(8,128)(2,1)S(1)} %copy-done.3), channel_id=1, source_target_pairs={{0,8},{8,16},{16,24},{24,0},{1,9},{9,17},{17,25},{25,1},{2,10},{10... | collective-permute-start | bytes 1572872 | tf_op jit(solution)/shard_map/ppermute | solution.py:25
  31.4 8.7 %collective-permute-start.7 = (bf16[4,32,1152]{2,1,0:T(8,128)(2,1)S(1)}, bf16[4,32,1152]{2,1,0:T(8,128)(2,1)S(1)}, u32[]{:S(2)}, u32[]{:S(2)}) collective-permute-start(bf16[4,32,1152]{2,1,0:T(8,128)(2,1)S(1)} %collective-permute-done.5.refs_0_), channel_id=1, source_target_pairs={{0,1},{1,2},{2,3},{3,4},{4,5},{5,6},{6,7},{7,0},{8,9},{9,10},{10,1... | collective-permute-start | bytes 884744 | tf_op jit(solution)/shard_map/ppermute | solution.py:25
  32.7 7.4 %collective-permute-start.8 = (bf16[4,32,1152]{2,1,0:T(8,128)(2,1)S(1)}, bf16[4,32,1152]{2,1,0:T(8,128)(2,1)S(1)}, u32[]{:S(2)}, u32[]{:S(2)}) collective-permute-start(bf16[4,32,1152]{2,1,0:T(8,128)(2,1)S(1)} %collective-permute-done.6.refs_1_), channel_id=1, source_target_pairs={{0,7},{1,0},{2,1},{3,2},{4,3},{5,4},{6,5},{7,6},{8,15},{9,8},{10,9... | collective-permute-start | bytes 884744 | tf_op jit(solution)/shard_map/ppermute | solution.py:25
  40.1 17.8 %collective-permute-start.16 = (bf16[5,32,1152]{2,1,0:T(8,128)(2,1)S(1)}, bf16[5,32,1152]{2,1,0:T(8,128)(2,1)S(1)}, u32[]{:S(2)}, u32[]{:S(2)}) collective-permute-start(bf16[5,32,1152]{2,1,0:T(8,128)(2,1)S(1)} %get-tuple-element.106), channel_id=1, source_target_pairs={{0,24},{8,0},{16,8},{24,16},{1,25},{9,1},{17,9},{25,17},{2,26},{10... | collective-permute-start | bytes 1105928 | tf_op jit(solution)/shard_map/ppermute | solution.py:25
  42.9 8.0 %collective-permute-start.11 = (bf16[2,32,1152]{2,1,0:T(8,128)(2,1)S(1)}, bf16[2,32,1152]{2,1,0:T(8,128)(2,1)S(1)}, u32[]{:S(2)}, u32[]{:S(2)}) collective-permute-start(bf16[2,32,1152]{2,1,0:T(8,128)(2,1)S(1)} %slice.21), channel_id=1, source_target_pairs={{0,1},{1,2},{2,3},{3,4},{4,5},{5,6},{6,7},{7,0},{8,9},{9,10},{10,1... | collective-permute-start | bytes 442376 | tf_op jit(solution)/shard_map/ppermute | solution.py:25
  44.2 6.7 %collective-permute-start.12 = (bf16[2,32,1152]{2,1,0:T(8,128)(2,1)S(1)}, bf16[2,32,1152]{2,1,0:T(8,128)(2,1)S(1)}, u32[]{:S(2)}, u32[]{:S(2)}) collective-permute-start(bf16[2,32,1152]{2,1,0:T(8,128)(2,1)S(1)} %slice.22), channel_id=1, source_target_pairs={{0,7},{1,0},{2,1},{3,2},{4,3},{5,4},{6,5},{7,6},{8,15},{9,8},{10,9... | collective-permute-start | bytes 442376 | tf_op jit(solution)/shard_map/ppermute | solution.py:25
  46.5 13.1 %collective-permute-start.17 = (bf16[5,32,1152]{2,1,0:T(8,128)(2,1)S(1)}, bf16[5,32,1152]{2,1,0:T(8,128)(2,1)S(1)}, u32[]{:S(2)}, u32[]{:S(2)}) collective-permute-start(bf16[5,32,1152]{2,1,0:T(8,128)(2,1)S(1)} %get-tuple-element.107), channel_id=1, source_target_pairs={{0,16},{8,24},{16,0},{24,8},{1,17},{9,25},{17,1},{25,9},{2,18},{10... | collective-permute-start | bytes 1105928 | tf_op jit(solution)/shard_map/ppermute | solution.py:25
  46.5 19.1 %collective-permute-start.18 = (bf16[5,32,1152]{2,1,0:T(8,128)(2,1)S(1)}, bf16[5,32,1152]{2,1,0:T(8,128)(2,1)S(1)}, u32[]{:S(2)}, u32[]{:S(2)}) collective-permute-start(bf16[5,32,1152]{2,1,0:T(8,128)(2,1)S(1)} %get-tuple-element.108), channel_id=1, source_target_pairs={{0,8},{8,16},{16,24},{24,0},{1,9},{9,17},{17,25},{25,1},{2,10},{10... | collective-permute-start | bytes 1105928 | tf_op jit(solution)/shard_map/ppermute | solution.py:25
  53.1 14.5 %collective-permute-start.13 = (bf16[3,32,1152]{2,1,0:T(8,128)(2,1)S(1)}, bf16[3,32,1152]{2,1,0:T(8,128)(2,1)S(1)}, u32[]{:S(2)}, u32[]{:S(2)}) collective-permute-start(bf16[3,32,1152]{2,1,0:T(8,128)(2,1)S(1)} %get-tuple-element.102), channel_id=1, source_target_pairs={{0,24},{8,0},{16,8},{24,16},{1,25},{9,1},{17,9},{25,17},{2,26},{10... | collective-permute-start | bytes 663560 | tf_op jit(solution)/shard_map/ppermute | solution.py:25
  55.5 13.1 %collective-permute-start.14 = (bf16[3,32,1152]{2,1,0:T(8,128)(2,1)S(1)}, bf16[3,32,1152]{2,1,0:T(8,128)(2,1)S(1)}, u32[]{:S(2)}, u32[]{:S(2)}) collective-permute-start(bf16[3,32,1152]{2,1,0:T(8,128)(2,1)S(1)} %get-tuple-element.103), channel_id=1, source_target_pairs={{0,16},{8,24},{16,0},{24,8},{1,17},{9,25},{17,1},{25,9},{2,18},{10... | collective-permute-start | bytes 663560 | tf_op jit(solution)/shard_map/ppermute | solution.py:25
  57.8 12.7 %collective-permute-start.15 = (bf16[3,32,1152]{2,1,0:T(8,128)(2,1)S(1)}, bf16[3,32,1152]{2,1,0:T(8,128)(2,1)S(1)}, u32[]{:S(2)}, u32[]{:S(2)}) collective-permute-start(bf16[3,32,1152]{2,1,0:T(8,128)(2,1)S(1)} %get-tuple-element.104), channel_id=1, source_target_pairs={{0,8},{8,16},{16,24},{24,0},{1,9},{9,17},{17,25},{25,1},{2,10},{10... | collective-permute-start | bytes 663560 | tf_op jit(solution)/shard_map/ppermute | solution.py:25
  72.5 19.7 %all-to-all-start = ((bf16[8,32,1152]{2,1,0:T(8,128)(2,1)}), bf16[8,32,1152]{2,1,0:T(8,128)(2,1)S(1)}, u32[]{:S(2)}, u32[]{:S(2)}) async-start(bf16[8,32,1152]{2,1,0:T(8,128)(2,1)} %get-tuple-element.112), calls=%async_computation | async-start | bytes 1179648 | tf_op jit(solution)/shard_map/all_to_all | solution.py:273
  78.0 10.7 %collective-permute-start.19 = (bf16[1024,256]{1,0:T(8,128)(2,1)S(1)}, bf16[1024,256]{1,0:T(8,128)(2,1)S(1)}, u32[]{:S(2)}, u32[]{:S(2)}) collective-permute-start(bf16[1024,256]{1,0:T(8,128)(2,1)S(1)} %copy-done.3), channel_id=1, source_target_pairs={{0,16},{8,24},{16,0},{24,8},{1,17},{9,25},{17,1},{25,9},{2,18},{10... | collective-permute-start | bytes 1572872 | tf_op jit(solution)/shard_map/ppermute | solution.py:25
  93.6 17.0 %all-to-all-start.1 = ((bf16[8,32,1024]{2,1,0:T(8,128)(2,1)}), bf16[8,32,1024]{2,1,0:T(8,128)(2,1)S(1)}, u32[]{:S(2)}, u32[]{:S(2)}) async-start(bf16[8,32,1024]{2,1,0:T(8,128)(2,1)} %finish.1), calls=%async_computation.1 | async-start | bytes 1048576 | tf_op jit(solution)/shard_map/all_to_all | solution.py:278
  113.9 5.8 %collective-permute-start.22 = (bf16[128,256]{1,0:T(8,128)(2,1)S(1)}, bf16[128,256]{1,0:T(8,128)(2,1)S(1)}, u32[]{:S(2)}, u32[]{:S(2)}) collective-permute-start(bf16[128,256]{1,0:T(8,128)(2,1)S(1)} %get-tuple-element.127), channel_id=1, source_target_pairs={{0,128},{64,192},{128,0},{192,64},{1,129},{65,193},{129,1},{193,65... | collective-permute-start | bytes 196616 | tf_op jit(solution)/shard_map/ppermute | solution.py:25
  116.4 5.5 %collective-permute-start.23 = (bf16[128,256]{1,0:T(8,128)(2,1)S(1)}, bf16[128,256]{1,0:T(8,128)(2,1)S(1)}, u32[]{:S(2)}, u32[]{:S(2)}) collective-permute-start(bf16[128,256]{1,0:T(8,128)(2,1)S(1)} %get-tuple-element.126), channel_id=1, source_target_pairs={{0,192},{64,0},{128,64},{192,128},{1,193},{65,1},{129,65},{193,129... | collective-permute-start | bytes 196616 | tf_op jit(solution)/shard_map/ppermute | solution.py:25
  121.9 9.5 %collective-permute-start.24 = (bf16[128,256]{1,0:T(8,128)(2,1)S(1)}, bf16[128,256]{1,0:T(8,128)(2,1)S(1)}, u32[]{:S(2)}, u32[]{:S(2)}) collective-permute-start(bf16[128,256]{1,0:T(8,128)(2,1)S(1)} %fusion.3), channel_id=1, source_target_pairs={{0,0},{8,64},{16,128},{24,192},{64,8},{72,72},{80,136},{88,200},{1... | collective-permute-start | bytes 196616 | tf_op jit(solution)/shard_map/ppermute | solution.py:294
  (7 other events, 36.1 us)

commit v2 on v1

--- a/solution.py
+++ b/solution.py
@@ -17,7 +17,6 @@
 EXP_SCALE = HEAD**-0.5 * math.log2(math.e)
 F32 = jnp.float32
 BF16 = jnp.bfloat16
-SUM_SENT = BF16
 VMEM_LIMIT = 28 * 1024 * 1024
 
 
@@ -217,13 +216,16 @@
             out_ref[copy, :, h * HEAD : (h + 1) * HEAD] = attn
 
 
+SUM_AT = (0, 2, 1, 3)
+
+
 def project_kernel(core_ref, turn_ref, attn_ref, *refs):
     w_refs, (keep_ref, give_ref) = refs[:4], refs[4:]
     core = core_ref[0]
     for out_ref, half in ((give_ref, 1 - core), (keep_ref, core)):
         rows = attn_ref[pl.ds(half * 4, 4)].reshape(-1, FLAT)
         for back, w_ref in enumerate(w_refs):
-            out_ref[lax.rem(turn_ref[0] - back + 8, 4)] = jnp.dot(
+            out_ref[lax.rem(turn_ref[0] + SUM_AT[back] + 4, 4)] = jnp.dot(
                 rows, w_ref[...], preferred_element_type=F32
             )
 
@@ -256,19 +258,23 @@
     weights = [shift(out_weight, "y", 4, step) for step in (1, 3)]
     low_2, high_2, near = tie((low_2, high_2, near))
     low_3, high_3 = shift(low_2, "z", 8, 1), shift(high_2, "z", 8, -1)
-    near = attend(me, [low_2, high_2], keys, values, near)
-    low_3, high_3, near, weights, out_weight = tie((low_3, high_3, near, weights, out_weight))
-    far = [shift(low_3[:2], "z", 8, 1), shift(high_3[2:], "z", 8, -1)]
     near = send(near)
-    beyond = attend(me, [low_3, high_3], keys, values)
-    far, beyond, out_weight = tie((far, beyond, out_weight))
-    beyond = send(attend(me, far, keys, values, beyond))
+    second = attend(me, [low_2, high_2], keys, values)
+    low_3, high_3, second, weights, out_weight = tie((low_3, high_3, second, weights, out_weight))
+    far = shift(low_3, "z", 8, 1)
+    second = send(second)
+    low_3, high_3, near = tie((low_3, high_3, near))
+    third = attend(me, [low_3, high_3], keys, values)
+    far, third, second, out_weight = tie((far, third, second, out_weight))
+    third = send(attend(me, [far], keys, values, third))
     weights = [out_weight, weights[0], shift(out_weight, "y", 4, 2), weights[1]]
 
     line = [jax.ShapeDtypeStruct((8, rows, WIDE), BF16), jax.ShapeDtypeStruct((rows, WIDE), F32)]
-    joined = local_call(functools.partial(line_kernel, [5], 0), "line", [my_z], near, line)
+    joined = local_call(
+        functools.partial(line_kernel, [3, 2], 0), "line", [my_z], [*near, *second], line
+    )
     joined, mine = local_call(
-        functools.partial(line_kernel, [3], 5), "line", [my_z], [*beyond, *joined], line
+        functools.partial(line_kernel, [3], 5), "line", [my_z], [*third, *joined], line
     )
     got = lax.all_to_all(joined, "z", 0, 0, tiled=True)
     got, weights = tie((got, weights))
@@ -289,8 +295,10 @@
     sums = keep + shift(give, "core", 2, 1)
     total = sums[0]
     for step in (1, 2, 3):
-        total = total + shift(sums[step].astype(SUM_SENT), "x", 4, step).astype(F32)
-    swap = [(a * 4 + b, b * 4 + a) for a in range(4) for b in range(4)]
+        total = total + shift(sums[step].astype(BF16), "x", 4, step).astype(F32)
+    swap = [
+        ((b + at) % 4 * 4 + b, b * 4 + (b - back) % 4) for b in range(4) for back, at in enumerate(SUM_AT)
+    ]
     return lax.ppermute(total.astype(BF16), ("x", "y"), swap)
 
 

time: 132 us -> 128 us (0.970)
  starting transfers between devices: 48.8 us -> 46.1 us
  waiting for transfers between devices: 56.4 us -> 54.6 us
    ppermute x24 -> x26, waiting for transfers between devices: 33.1 us -> 31.7 us  [shift(): return lax.ppermute(x, axis, [(i, (i + step) % size) for i in range(size)])]
    ppermute x24 -> x26, starting transfers between devices: 36.7 us -> 35.9 us  [shift(): return lax.ppermute(x, axis, [(i, (i + step) % size) for i in range(size)])]
  transfers between devices with their start and end apart: 27 -> 29, of which waited for: 16 -> 17; matrix products, arithmetic and copies ran while one was open for 0% -> 0% of each run, Pallas kernels for 13% -> 11%
where the time goes in v2:
time: 128 us; the launch traced here: 127 us
  waiting for transfers between devices  54.6 us (43%)
  starting transfers between devices  46.1 us (36%)
  Pallas kernels  20.7 us (16%)
  local copies, waits for them, and re-layouts  4.78 us (4%)
    ppermute x26, starting transfers between devices, shift(): return lax.ppermute(x, axis, [(i, (i + step) % size) for i in range(size)])  35.9 us
    ppermute x26, waiting for transfers between devices, shift(): return lax.ppermute(x, axis, [(i, (i + step) % size) for i in range(size)])  31.7 us
    pallas_call x9, Pallas kernels, local_call(): pl.pallas_call(kernel, out_shape=out_shape, in_specs=[pl.BlockSpec(memory...  20.7 us
    all_to_all x1, waiting for transfers between devices, per_device(): attn = lax.all_to_all(attn, 'z', 0, 0, tiled=True)  13.3 us
    ppermute x1, waiting for transfers between devices, per_device(): return lax.ppermute(total.astype(BF16), ('x', 'y'), swap)  6.34 us
    unnamed x10, local copies, waits for them, and re-layouts  4.67 us
    all_to_all x1, starting transfers between devices, per_device(): got = lax.all_to_all(joined, 'z', 0, 0, tiled=True)  4.38 us
    all_to_all x1, starting transfers between devices, per_device(): attn = lax.all_to_all(attn, 'z', 0, 0, tiled=True)  3.9 us
  transfers between devices with their start and end apart: 29, of which 17 were waited for; matrix products, arithmetic and copies ran while one was open for 0% of the time, Pallas kernels for 11%

profile of v2, /device:TPU:6, one launch (start us, length us, event | category | flops | bytes accessed | tf_op | source)
XLA Modules:
  0.0 127.3 jit_solution(9840222587973116053)
XLA Ops:
  1.8 3.1 %collective-permute-start.2 = (bf16[32,1152]{1,0:T(8,128)(2,1)S(1)}, bf16[32,1152]{1,0:T(8,128)(2,1)S(1)}, u32[]{:S(2)}, u32[]{:S(2)}) collective-permute-start(bf16[32,1152]{1,0:T(8,128)(2,1)S(1)} %concatenate.3), channel_id=1, source_target_pairs={{0,24},{8,0},{16,8},{24,16},{1,25},{9,1},{17,9},{25,17},{2,26},{10... | collective-permute-start | bytes 221192 | tf_op jit(solution)/shard_map/ppermute | solution.py:24
  7.3 3.6 %collective-permute-done.1 = bf16[32,1152]{1,0:T(8,128)(2,1)S(1)} collective-permute-done((bf16[32,1152]{1,0:T(8,128)(2,1)S(1)}, bf16[32,1152]{1,0:T(8,128)(2,1)S(1)}, u32[]{:S(2)}, u32[]{:S(2)}) %collective-permute-start.1) | collective-permute-done | bytes 73760 | tf_op jit(solution)/shard_map/ppermute | solution.py:24
  11.7 5.9 %collective-permute-start.4 = (bf16[4,32,1152]{2,1,0:T(8,128)(2,1)S(1)}, bf16[4,32,1152]{2,1,0:T(8,128)(2,1)S(1)}, u32[]{:S(2)}, u32[]{:S(2)}) collective-permute-start(bf16[4,32,1152]{2,1,0:T(8,128)(2,1)S(1)} %pad_maximum_fusion.refs_0_), channel_id=1, source_target_pairs={{0,7},{1,0},{2,1},{3,2},{4,3},{5,4},{6,5},{7,6},{8,15},{9,8},{10,9... | collective-permute-start | bytes 884744 | tf_op jit(solution)/shard_map/ppermute | solution.py:24
  17.6 3.2 %collective-permute-start.10 = (bf16[1024,256]{1,0:T(8,128)(2,1)}, bf16[1024,256]{1,0:T(8,128)(2,1)S(1)}, u32[]{:S(2)}, u32[]{:S(2)}) collective-permute-start(bf16[1024,256]{1,0:T(8,128)(2,1)} %refs_0_), channel_id=1, source_target_pairs={{0,24},{8,0},{16,8},{24,16},{1,25},{9,1},{17,9},{25,17},{2,26},{10... | collective-permute-start | bytes 1572872 | tf_op jit(solution)/shard_map/ppermute | solution.py:24
  24.1 2.0 %attend.5 = (f32[1,32,1152]{2,1,0:T(8,128)S(1)}, bf16[1,32,1152]{2,1,0:T(8,128)(2,1)S(1)}, bf16[1,32,1152]{2,1,0:T(8,128)(2,1)S(1)}, bf16[1,32,1152]{2,1,0:T(8,128)(2,1)S(1)}) custom-call(s32[1]{0:T(128)} %bitcast.3.me_ref, bf16[4,32,1152]{2,1,0:T(8,128)(2,1)S(1)} %pad_maximum_fusion.refs_0_, bf16[16,512,128]{2,1,0:T(8,128)(2,1)S(1)} %bitcast.31, ...), custom_call_target="tpu_custom_call" | custom-call | flops 536870912 | bytes 4857856 | tf_op jit(solution)/shard_map/attend/pallas_call | solution.py:133
  26.2 3.3 %collective-permute-start.6 = (bf16[4,32,1152]{2,1,0:T(8,128)(2,1)S(1)}, bf16[4,32,1152]{2,1,0:T(8,128)(2,1)S(1)}, u32[]{:S(2)}, u32[]{:S(2)}) collective-permute-start(bf16[4,32,1152]{2,1,0:T(8,128)(2,1)S(1)} %collective-permute-done.4.refs_1_), channel_id=1, source_target_pairs={{0,7},{1,0},{2,1},{3,2},{4,3},{5,4},{6,5},{7,6},{8,15},{9,8},{10,9... | collective-permute-start | bytes 884744 | tf_op jit(solution)/shard_map/ppermute | solution.py:24
  29.5 3.5 %attend.6 = (f32[3,32,1152]{2,1,0:T(8,128)S(1)}, bf16[3,32,1152]{2,1,0:T(8,128)(2,1)S(1)}, bf16[3,32,1152]{2,1,0:T(8,128)(2,1)S(1)}, bf16[3,32,1152]{2,1,0:T(8,128)(2,1)S(1)}) custom-call(s32[1]{0:T(128)} %bitcast.3.me_ref, bf16[4,32,1152]{2,1,0:T(8,128)(2,1)S(1)} %collective-permute-done.3.refs_0_, bf16[4,32,1152]{2,1,0:T(8,128)(2,1)S(1)} %collective-permute-done.4.refs_1_, ...), custom_call_target="tpu_custom_call" | custom-call | flops 1073741824 | bytes 6258688 | tf_op jit(solution)/shard_map/attend/pallas_call | solution.py:133
  34.2 3.3 %collective-permute-start.8 = (bf16[4,32,1152]{2,1,0:T(8,128)(2,1)S(1)}, bf16[4,32,1152]{2,1,0:T(8,128)(2,1)S(1)}, u32[]{:S(2)}, u32[]{:S(2)}) collective-permute-start(bf16[4,32,1152]{2,1,0:T(8,128)(2,1)S(1)} %collective-permute-done.6.refs_1_), channel_id=1, source_target_pairs={{0,7},{1,0},{2,1},{3,2},{4,3},{5,4},{6,5},{7,6},{8,15},{9,8},{10,9... | collective-permute-start | bytes 884744 | tf_op jit(solution)/shard_map/ppermute | solution.py:24
  40.1 3.5 %attend.7 = (f32[2,32,1152]{2,1,0:T(8,128)S(1)}, bf16[2,32,1152]{2,1,0:T(8,128)(2,1)S(1)}, bf16[2,32,1152]{2,1,0:T(8,128)(2,1)S(1)}, bf16[2,32,1152]{2,1,0:T(8,128)(2,1)S(1)}) custom-call(s32[1]{0:T(128)} %bitcast.3.me_ref, bf16[4,32,1152]{2,1,0:T(8,128)(2,1)S(1)} %collective-permute-done.5.refs_0_, bf16[4,32,1152]{2,1,0:T(8,128)(2,1)S(1)} %collective-permute-done.6.refs_1_, ...), custom_call_target="tpu_custom_call" | custom-call | flops 1073741824 | bytes 5521408 | tf_op jit(solution)/shard_map/attend/pallas_call | solution.py:133
  43.9 2.0 %collective-permute-start.15 = (bf16[2,32,1152]{2,1,0:T(8,128)(2,1)S(1)}, bf16[2,32,1152]{2,1,0:T(8,128)(2,1)S(1)}, u32[]{:S(2)}, u32[]{:S(2)}) collective-permute-start(bf16[2,32,1152]{2,1,0:T(8,128)(2,1)S(1)} %get-tuple-element.106), channel_id=1, source_target_pairs={{0,24},{8,0},{16,8},{24,16},{1,25},{9,1},{17,9},{25,17},{2,26},{10... | collective-permute-start | bytes 442376 | tf_op jit(solution)/shard_map/ppermute | solution.py:24
  50.8 3.5 %attend.8 = (f32[2,32,1152]{2,1,0:T(8,128)S(1)}, bf16[2,32,1152]{2,1,0:T(8,128)(2,1)S(1)}, bf16[2,32,1152]{2,1,0:T(8,128)(2,1)S(1)}, bf16[2,32,1152]{2,1,0:T(8,128)(2,1)S(1)}) custom-call(s32[1]{0:T(128)} %bitcast.3.me_ref, bf16[4,32,1152]{2,1,0:T(8,128)(2,1)S(1)} %collective-permute-done.7.refs_0_, bf16[4,32,1152]{2,1,0:T(8,128)(2,1)S(1)} %collective-permute-done.8.refs_1_, ...), custom_call_target="tpu_custom_call" | custom-call | flops 1073741824 | bytes 5521408 | tf_op jit(solution)/shard_map/attend/pallas_call | solution.py:133
  55.0 2.1 %attend.9 = (f32[3,32,1152]{2,1,0:T(8,128)S(1)}, bf16[3,32,1152]{2,1,0:T(8,128)(2,1)S(1)}, bf16[3,32,1152]{2,1,0:T(8,128)(2,1)S(1)}, bf16[3,32,1152]{2,1,0:T(8,128)(2,1)S(1)}) custom-call(s32[1]{0:T(128)} %bitcast.3.me_ref, bf16[4,32,1152]{2,1,0:T(8,128)(2,1)S(1)} %collective-permute-done.11.refs_0_, bf16[16,512,128]{2,1,0:T(8,128)(2,1)S(1)} %bitcast.35, ...), custom_call_target="tpu_custom_call" | custom-call | flops 536870912 | bytes 6332416 | tf_op jit(solution)/shard_map/attend/pallas_call | solution.py:133
  57.1 2.1 %collective-permute-start.18 = (bf16[3,32,1152]{2,1,0:T(8,128)(2,1)S(1)}, bf16[3,32,1152]{2,1,0:T(8,128)(2,1)S(1)}, u32[]{:S(2)}, u32[]{:S(2)}) collective-permute-start(bf16[3,32,1152]{2,1,0:T(8,128)(2,1)S(1)} %get-tuple-element.116), channel_id=1, source_target_pairs={{0,24},{8,0},{16,8},{24,16},{1,25},{9,1},{17,9},{25,17},{2,26},{10... | collective-permute-start | bytes 663560 | tf_op jit(solution)/shard_map/ppermute | solution.py:24
  60.5 1.9 %line.2 = (bf16[8,32,1152]{2,1,0:T(8,128)(2,1)S(1)}, f32[32,1152]{1,0:T(8,128)S(1)}) custom-call(s32[1]{0:T(128)} %bitcast.2.z_ref, f32[3,32,1152]{2,1,0:T(8,128)S(1)} %get-tuple-element.119.refs_0_, bf16[3,32,1152]{2,1,0:T(8,128)(2,1)S(1)} %collective-permute-done.12.refs_1_, bf16[3,32,1152]{2,1,0:T(8,128)(2,1)S(1)} %collective-permute-done.13.refs_2_, ...), custom_call_target="tpu_custom_call" | custom-call | bytes 2580480 | tf_op jit(solution)/shard_map/line/pallas_call | solution.py:133
  62.5 2.6 %collective-permute-done.18.refs_1_ = bf16[3,32,1152]{2,1,0:T(8,128)(2,1)S(1)} collective-permute-done((bf16[3,32,1152]{2,1,0:T(8,128)(2,1)S(1)}, bf16[3,32,1152]{2,1,0:T(8,128)(2,1)S(1)}, u32[]{:S(2)}, u32[]{:S(2)}) %collective-permute-start.18) | collective-permute-done | bytes 221216 | tf_op jit(solution)/shard_map/ppermute | solution.py:24
  66.8 2.0 %collective-permute-done.20.refs_3_ = bf16[3,32,1152]{2,1,0:T(8,128)(2,1)S(1)} collective-permute-done((bf16[3,32,1152]{2,1,0:T(8,128)(2,1)S(1)}, bf16[3,32,1152]{2,1,0:T(8,128)(2,1)S(1)}, u32[]{:S(2)}, u32[]{:S(2)}) %collective-permute-start.20) | collective-permute-done | bytes 221216 | tf_op jit(solution)/shard_map/ppermute | solution.py:24
  68.7 1.9 %line.3 = (bf16[8,32,1152]{2,1,0:T(8,128)(2,1)}, f32[32,1152]{1,0:T(8,128)S(1)}) custom-call(s32[1]{0:T(128)} %bitcast.2.z_ref, f32[3,32,1152]{2,1,0:T(8,128)S(1)} %get-tuple-element.115.refs_0_, bf16[3,32,1152]{2,1,0:T(8,128)(2,1)S(1)} %collective-permute-done.18.refs_1_, bf16[3,32,1152]{2,1,0:T(8,128)(2,1)S(1)} %collective-permute-done.19.refs_2_, ...), custom_call_target="tpu_custom_call" | custom-call | bytes 2580480 | tf_op jit(solution)/shard_map/line/pallas_call | solution.py:133
  70.7 4.4 %all-to-all-start = ((bf16[8,32,1152]{2,1,0:T(8,128)(2,1)}), bf16[8,32,1152]{2,1,0:T(8,128)(2,1)S(1)}, u32[]{:S(2)}, u32[]{:S(2)}) async-start(bf16[8,32,1152]{2,1,0:T(8,128)(2,1)} %get-tuple-element.130), calls=%async_computation | async-start | bytes 1179648 | tf_op jit(solution)/shard_map/all_to_all | solution.py:279
  75.4 10.4 %collective-permute-done.21.refs_2_ = bf16[1024,256]{1,0:T(8,128)(2,1)S(1)} collective-permute-done((bf16[1024,256]{1,0:T(8,128)(2,1)S(1)}, bf16[1024,256]{1,0:T(8,128)(2,1)S(1)}, u32[]{:S(2)}, u32[]{:S(2)}) %collective-permute-start.21) | collective-permute-done | bytes 524320 | tf_op jit(solution)/shard_map/ppermute | solution.py:24
  85.8 3.2 %all-to-all-done.got_ref = bf16[8,32,1152]{2,1,0:T(8,128)(2,1)S(1)} async-done(((bf16[8,32,1152]{2,1,0:T(8,128)(2,1)}), bf16[8,32,1152]{2,1,0:T(8,128)(2,1)S(1)}, u32[]{:S(2)}, u32[]{:S(2)}) %all-to-all-start) | async-done | bytes 589856 | tf_op jit(solution)/shard_map/all_to_all | solution.py:279
  90.4 3.9 %all-to-all-start.1 = ((bf16[8,32,1024]{2,1,0:T(8,128)(2,1)}), bf16[8,32,1024]{2,1,0:T(8,128)(2,1)S(1)}, u32[]{:S(2)}, u32[]{:S(2)}) async-start(bf16[8,32,1024]{2,1,0:T(8,128)(2,1)} %finish.1), calls=%async_computation.1 | async-start | bytes 1048576 | tf_op jit(solution)/shard_map/all_to_all | solution.py:284
  94.3 13.3 %all-to-all-done.1.attn_ref = bf16[8,32,1024]{2,1,0:T(8,128)(2,1)S(1)} async-done(((bf16[8,32,1024]{2,1,0:T(8,128)(2,1)}), bf16[8,32,1024]{2,1,0:T(8,128)(2,1)S(1)}, u32[]{:S(2)}, u32[]{:S(2)}) %all-to-all-start.1) | async-done | bytes 524320 | tf_op jit(solution)/shard_map/all_to_all | solution.py:284
  114.8 2.4 %collective-permute-done.25 = bf16[128,256]{1,0:T(8,128)(2,1)S(1)} collective-permute-done((bf16[128,256]{1,0:T(8,128)(2,1)S(1)}, bf16[128,256]{1,0:T(8,128)(2,1)S(1)}, u32[]{:S(2)}, u32[]{:S(2)}) %collective-permute-start.25) | collective-permute-done | bytes 65568 | tf_op jit(solution)/shard_map/ppermute | solution.py:24
  120.3 6.3 %collective-permute-done.26 = bf16[128,256]{1,0:T(8,128)(2,1)S(1)} collective-permute-done((bf16[128,256]{1,0:T(8,128)(2,1)S(1)}, bf16[128,256]{1,0:T(8,128)(2,1)S(1)}, u32[]{:S(2)}, u32[]{:S(2)}) %collective-permute-start.26) | collective-permute-done | bytes 65568 | tf_op jit(solution)/shard_map/ppermute | solution.py:302
  (60 shorter events, 33.5 us)
Async XLA Ops:
  5.5 6.2 %collective-permute-start = (bf16[32,1152]{1,0:T(8,128)(2,1)S(1)}, bf16[32,1152]{1,0:T(8,128)(2,1)S(1)}, u32[]{:S(2)}, u32[]{:S(2)}) collective-permute-start(bf16[32,1152]{1,0:T(8,128)(2,1)S(1)} %concatenate.3), channel_id=1, source_target_pairs={{0,8},{8,16},{16,24},{24,0},{1,9},{9,17},{17,25},{25,1},{2,10},{10... | collective-permute-start | bytes 221192 | tf_op jit(solution)/shard_map/ppermute | solution.py:24
  11.7 14.4 %collective-permute-start.4 = (bf16[4,32,1152]{2,1,0:T(8,128)(2,1)S(1)}, bf16[4,32,1152]{2,1,0:T(8,128)(2,1)S(1)}, u32[]{:S(2)}, u32[]{:S(2)}) collective-permute-start(bf16[4,32,1152]{2,1,0:T(8,128)(2,1)S(1)} %pad_maximum_fusion.refs_0_), channel_id=1, source_target_pairs={{0,7},{1,0},{2,1},{3,2},{4,3},{5,4},{6,5},{7,6},{8,15},{9,8},{10,9... | collective-permute-start | bytes 884744 | tf_op jit(solution)/shard_map/ppermute | solution.py:24
  17.6 8.5 %collective-permute-start.3 = (bf16[4,32,1152]{2,1,0:T(8,128)(2,1)S(1)}, bf16[4,32,1152]{2,1,0:T(8,128)(2,1)S(1)}, u32[]{:S(2)}, u32[]{:S(2)}) collective-permute-start(bf16[4,32,1152]{2,1,0:T(8,128)(2,1)S(1)} %pad_maximum_fusion.refs_0_), channel_id=1, source_target_pairs={{0,1},{1,2},{2,3},{3,4},{4,5},{5,6},{6,7},{7,0},{8,9},{9,10},{10,1... | collective-permute-start | bytes 884744 | tf_op jit(solution)/shard_map/ppermute | solution.py:24
  17.6 20.2 %collective-permute-start.9 = (bf16[1024,256]{1,0:T(8,128)(2,1)}, bf16[1024,256]{1,0:T(8,128)(2,1)S(1)}, u32[]{:S(2)}, u32[]{:S(2)}) collective-permute-start(bf16[1024,256]{1,0:T(8,128)(2,1)} %refs_0_), channel_id=1, source_target_pairs={{0,8},{8,16},{16,24},{24,0},{1,9},{9,17},{17,25},{25,1},{2,10},{10... | collective-permute-start | bytes 1572872 | tf_op jit(solution)/shard_map/ppermute | solution.py:24
  17.6 21.0 %collective-permute-start.10 = (bf16[1024,256]{1,0:T(8,128)(2,1)}, bf16[1024,256]{1,0:T(8,128)(2,1)S(1)}, u32[]{:S(2)}, u32[]{:S(2)}) collective-permute-start(bf16[1024,256]{1,0:T(8,128)(2,1)} %refs_0_), channel_id=1, source_target_pairs={{0,24},{8,0},{16,8},{24,16},{1,25},{9,1},{17,9},{25,17},{2,26},{10... | collective-permute-start | bytes 1572872 | tf_op jit(solution)/shard_map/ppermute | solution.py:24
  26.1 8.0 %collective-permute-start.5 = (bf16[4,32,1152]{2,1,0:T(8,128)(2,1)S(1)}, bf16[4,32,1152]{2,1,0:T(8,128)(2,1)S(1)}, u32[]{:S(2)}, u32[]{:S(2)}) collective-permute-start(bf16[4,32,1152]{2,1,0:T(8,128)(2,1)S(1)} %collective-permute-done.3.refs_0_), channel_id=1, source_target_pairs={{0,1},{1,2},{2,3},{3,4},{4,5},{5,6},{6,7},{7,0},{8,9},{9,10},{10,1... | collective-permute-start | bytes 884744 | tf_op jit(solution)/shard_map/ppermute | solution.py:24
  26.2 7.9 %collective-permute-start.6 = (bf16[4,32,1152]{2,1,0:T(8,128)(2,1)S(1)}, bf16[4,32,1152]{2,1,0:T(8,128)(2,1)S(1)}, u32[]{:S(2)}, u32[]{:S(2)}) collective-permute-start(bf16[4,32,1152]{2,1,0:T(8,128)(2,1)S(1)} %collective-permute-done.4.refs_1_), channel_id=1, source_target_pairs={{0,7},{1,0},{2,1},{3,2},{4,3},{5,4},{6,5},{7,6},{8,15},{9,8},{10,9... | collective-permute-start | bytes 884744 | tf_op jit(solution)/shard_map/ppermute | solution.py:24
  34.1 9.5 %collective-permute-start.7 = (bf16[4,32,1152]{2,1,0:T(8,128)(2,1)S(1)}, bf16[4,32,1152]{2,1,0:T(8,128)(2,1)S(1)}, u32[]{:S(2)}, u32[]{:S(2)}) collective-permute-start(bf16[4,32,1152]{2,1,0:T(8,128)(2,1)S(1)} %collective-permute-done.5.refs_0_), channel_id=1, source_target_pairs={{0,1},{1,2},{2,3},{3,4},{4,5},{5,6},{6,7},{7,0},{8,9},{9,10},{10,1... | collective-permute-start | bytes 884744 | tf_op jit(solution)/shard_map/ppermute | solution.py:24
  34.2 9.5 %collective-permute-start.8 = (bf16[4,32,1152]{2,1,0:T(8,128)(2,1)S(1)}, bf16[4,32,1152]{2,1,0:T(8,128)(2,1)S(1)}, u32[]{:S(2)}, u32[]{:S(2)}) collective-permute-start(bf16[4,32,1152]{2,1,0:T(8,128)(2,1)S(1)} %collective-permute-done.6.refs_1_), channel_id=1, source_target_pairs={{0,7},{1,0},{2,1},{3,2},{4,3},{5,4},{6,5},{7,6},{8,15},{9,8},{10,9... | collective-permute-start | bytes 884744 | tf_op jit(solution)/shard_map/ppermute | solution.py:24
  37.5 8.4 %collective-permute-start.12 = (bf16[3,32,1152]{2,1,0:T(8,128)(2,1)S(1)}, bf16[3,32,1152]{2,1,0:T(8,128)(2,1)S(1)}, u32[]{:S(2)}, u32[]{:S(2)}) collective-permute-start(bf16[3,32,1152]{2,1,0:T(8,128)(2,1)S(1)} %get-tuple-element.96), channel_id=1, source_target_pairs={{0,24},{8,0},{16,8},{24,16},{1,25},{9,1},{17,9},{25,17},{2,26},{10... | collective-permute-start | bytes 663560 | tf_op jit(solution)/shard_map/ppermute | solution.py:24
  37.9 9.6 %collective-permute-start.13 = (bf16[3,32,1152]{2,1,0:T(8,128)(2,1)S(1)}, bf16[3,32,1152]{2,1,0:T(8,128)(2,1)S(1)}, u32[]{:S(2)}, u32[]{:S(2)}) collective-permute-start(bf16[3,32,1152]{2,1,0:T(8,128)(2,1)S(1)} %get-tuple-element.97), channel_id=1, source_target_pairs={{0,16},{8,24},{16,0},{24,8},{1,17},{9,25},{17,1},{25,9},{2,18},{10... | collective-permute-start | bytes 663560 | tf_op jit(solution)/shard_map/ppermute | solution.py:24
  38.6 12.1 %collective-permute-start.14 = (bf16[3,32,1152]{2,1,0:T(8,128)(2,1)S(1)}, bf16[3,32,1152]{2,1,0:T(8,128)(2,1)S(1)}, u32[]{:S(2)}, u32[]{:S(2)}) collective-permute-start(bf16[3,32,1152]{2,1,0:T(8,128)(2,1)S(1)} %get-tuple-element.98), channel_id=1, source_target_pairs={{0,8},{8,16},{16,24},{24,0},{1,9},{9,17},{17,25},{25,1},{2,10},{10... | collective-permute-start | bytes 663560 | tf_op jit(solution)/shard_map/ppermute | solution.py:24
  43.6 11.4 %collective-permute-start.11 = (bf16[4,32,1152]{2,1,0:T(8,128)(2,1)S(1)}, bf16[4,32,1152]{2,1,0:T(8,128)(2,1)S(1)}, u32[]{:S(2)}, u32[]{:S(2)}) collective-permute-start(bf16[4,32,1152]{2,1,0:T(8,128)(2,1)S(1)} %collective-permute-done.7.refs_0_), channel_id=1, source_target_pairs={{0,1},{1,2},{2,3},{3,4},{4,5},{5,6},{6,7},{7,0},{8,9},{9,10},{10,1... | collective-permute-start | bytes 884744 | tf_op jit(solution)/shard_map/ppermute | solution.py:24
  43.9 10.4 %collective-permute-start.15 = (bf16[2,32,1152]{2,1,0:T(8,128)(2,1)S(1)}, bf16[2,32,1152]{2,1,0:T(8,128)(2,1)S(1)}, u32[]{:S(2)}, u32[]{:S(2)}) collective-permute-start(bf16[2,32,1152]{2,1,0:T(8,128)(2,1)S(1)} %get-tuple-element.106), channel_id=1, source_target_pairs={{0,24},{8,0},{16,8},{24,16},{1,25},{9,1},{17,9},{25,17},{2,26},{10... | collective-permute-start | bytes 442376 | tf_op jit(solution)/shard_map/ppermute | solution.py:24
  45.9 8.4 %collective-permute-start.16 = (bf16[2,32,1152]{2,1,0:T(8,128)(2,1)S(1)}, bf16[2,32,1152]{2,1,0:T(8,128)(2,1)S(1)}, u32[]{:S(2)}, u32[]{:S(2)}) collective-permute-start(bf16[2,32,1152]{2,1,0:T(8,128)(2,1)S(1)} %get-tuple-element.107), channel_id=1, source_target_pairs={{0,16},{8,24},{16,0},{24,8},{1,17},{9,25},{17,1},{25,9},{2,18},{10... | collective-permute-start | bytes 442376 | tf_op jit(solution)/shard_map/ppermute | solution.py:24
  47.5 7.5 %collective-permute-start.17 = (bf16[2,32,1152]{2,1,0:T(8,128)(2,1)S(1)}, bf16[2,32,1152]{2,1,0:T(8,128)(2,1)S(1)}, u32[]{:S(2)}, u32[]{:S(2)}) collective-permute-start(bf16[2,32,1152]{2,1,0:T(8,128)(2,1)S(1)} %get-tuple-element.108), channel_id=1, source_target_pairs={{0,8},{8,16},{16,24},{24,0},{1,9},{9,17},{17,25},{25,1},{2,10},{10... | collective-permute-start | bytes 442376 | tf_op jit(solution)/shard_map/ppermute | solution.py:24
  57.1 8.0 %collective-permute-start.18 = (bf16[3,32,1152]{2,1,0:T(8,128)(2,1)S(1)}, bf16[3,32,1152]{2,1,0:T(8,128)(2,1)S(1)}, u32[]{:S(2)}, u32[]{:S(2)}) collective-permute-start(bf16[3,32,1152]{2,1,0:T(8,128)(2,1)S(1)} %get-tuple-element.116), channel_id=1, source_target_pairs={{0,24},{8,0},{16,8},{24,16},{1,25},{9,1},{17,9},{25,17},{2,26},{10... | collective-permute-start | bytes 663560 | tf_op jit(solution)/shard_map/ppermute | solution.py:24
  59.2 7.5 %collective-permute-start.19 = (bf16[3,32,1152]{2,1,0:T(8,128)(2,1)S(1)}, bf16[3,32,1152]{2,1,0:T(8,128)(2,1)S(1)}, u32[]{:S(2)}, u32[]{:S(2)}) collective-permute-start(bf16[3,32,1152]{2,1,0:T(8,128)(2,1)S(1)} %get-tuple-element.117), channel_id=1, source_target_pairs={{0,16},{8,24},{16,0},{24,8},{1,17},{9,25},{17,1},{25,9},{2,18},{10... | collective-permute-start | bytes 663560 | tf_op jit(solution)/shard_map/ppermute | solution.py:24
  59.2 9.5 %collective-permute-start.20 = (bf16[3,32,1152]{2,1,0:T(8,128)(2,1)S(1)}, bf16[3,32,1152]{2,1,0:T(8,128)(2,1)S(1)}, u32[]{:S(2)}, u32[]{:S(2)}) collective-permute-start(bf16[3,32,1152]{2,1,0:T(8,128)(2,1)S(1)} %get-tuple-element.118), channel_id=1, source_target_pairs={{0,8},{8,16},{16,24},{24,0},{1,9},{9,17},{17,25},{25,1},{2,10},{10... | collective-permute-start | bytes 663560 | tf_op jit(solution)/shard_map/ppermute | solution.py:24
  70.7 18.4 %all-to-all-start = ((bf16[8,32,1152]{2,1,0:T(8,128)(2,1)}), bf16[8,32,1152]{2,1,0:T(8,128)(2,1)S(1)}, u32[]{:S(2)}, u32[]{:S(2)}) async-start(bf16[8,32,1152]{2,1,0:T(8,128)(2,1)} %get-tuple-element.130), calls=%async_computation | async-start | bytes 1179648 | tf_op jit(solution)/shard_map/all_to_all | solution.py:279
  75.1 10.8 %collective-permute-start.21 = (bf16[1024,256]{1,0:T(8,128)(2,1)S(1)}, bf16[1024,256]{1,0:T(8,128)(2,1)S(1)}, u32[]{:S(2)}, u32[]{:S(2)}) collective-permute-start(bf16[1024,256]{1,0:T(8,128)(2,1)S(1)} %copy-done.3), channel_id=1, source_target_pairs={{0,16},{8,24},{16,0},{24,8},{1,17},{9,25},{17,1},{25,9},{2,18},{10... | collective-permute-start | bytes 1572872 | tf_op jit(solution)/shard_map/ppermute | solution.py:24
  90.4 17.2 %all-to-all-start.1 = ((bf16[8,32,1024]{2,1,0:T(8,128)(2,1)}), bf16[8,32,1024]{2,1,0:T(8,128)(2,1)S(1)}, u32[]{:S(2)}, u32[]{:S(2)}) async-start(bf16[8,32,1024]{2,1,0:T(8,128)(2,1)} %finish.1), calls=%async_computation.1 | async-start | bytes 1048576 | tf_op jit(solution)/shard_map/all_to_all | solution.py:284
  111.0 6.2 %collective-permute-start.25 = (bf16[128,256]{1,0:T(8,128)(2,1)S(1)}, bf16[128,256]{1,0:T(8,128)(2,1)S(1)}, u32[]{:S(2)}, u32[]{:S(2)}) collective-permute-start(bf16[128,256]{1,0:T(8,128)(2,1)S(1)} %get-tuple-element.144), channel_id=1, source_target_pairs={{0,192},{64,0},{128,64},{192,128},{1,193},{65,1},{129,65},{193,129... | collective-permute-start | bytes 196616 | tf_op jit(solution)/shard_map/ppermute | solution.py:24
  118.4 8.3 %collective-permute-start.26 = (bf16[128,256]{1,0:T(8,128)(2,1)S(1)}, bf16[128,256]{1,0:T(8,128)(2,1)S(1)}, u32[]{:S(2)}, u32[]{:S(2)}) collective-permute-start(bf16[128,256]{1,0:T(8,128)(2,1)S(1)} %fusion.3), channel_id=1, source_target_pairs={{0,0},{128,24},{64,16},{192,8},{72,72},{200,64},{136,88},{8,80},{1... | collective-permute-start | bytes 196616 | tf_op jit(solution)/shard_map/ppermute | solution.py:302
  (9 other events, 58.1 us)

commit v3 on v2

--- a/solution.py
+++ b/solution.py
@@ -216,7 +216,7 @@
             out_ref[copy, :, h * HEAD : (h + 1) * HEAD] = attn
 
 
-SUM_AT = (0, 2, 1, 3)
+SUM_AT = (2, 3, 0, 1)
 
 
 def project_kernel(core_ref, turn_ref, attn_ref, *refs):
@@ -255,19 +255,18 @@
     low_1, high_1, near = tie((low_1, high_1, near))
     low_2, high_2 = shift(low_1, "z", 8, 1), shift(high_1, "z", 8, -1)
     near = attend(me, [low_1, high_1], keys, values, near)
-    weights = [shift(out_weight, "y", 4, step) for step in (1, 3)]
     low_2, high_2, near = tie((low_2, high_2, near))
     low_3, high_3 = shift(low_2, "z", 8, 1), shift(high_2, "z", 8, -1)
     near = send(near)
     second = attend(me, [low_2, high_2], keys, values)
-    low_3, high_3, second, weights, out_weight = tie((low_3, high_3, second, weights, out_weight))
+    low_3, high_3, second = tie((low_3, high_3, second))
     far = shift(low_3, "z", 8, 1)
     second = send(second)
     low_3, high_3, near = tie((low_3, high_3, near))
     third = attend(me, [low_3, high_3], keys, values)
     far, third, second, out_weight = tie((far, third, second, out_weight))
     third = send(attend(me, [far], keys, values, third))
-    weights = [out_weight, weights[0], shift(out_weight, "y", 4, 2), weights[1]]
+    across = shift(out_weight, "y", 4, 2)
 
     line = [jax.ShapeDtypeStruct((8, rows, WIDE), BF16), jax.ShapeDtypeStruct((rows, WIDE), F32)]
     joined = local_call(
@@ -277,11 +276,13 @@
         functools.partial(line_kernel, [3], 5), "line", [my_z], [*third, *joined], line
     )
     got = lax.all_to_all(joined, "z", 0, 0, tiled=True)
-    got, weights = tie((got, weights))
+    got, across = tie((got, across))
     (attn,) = local_call(
         finish_kernel, "finish", [my_z], [mine, got], [jax.ShapeDtypeStruct((8, rows, FLAT), BF16)]
     )
+    attn, out_weight = tie((attn, out_weight))
     attn = lax.all_to_all(attn, "z", 0, 0, tiled=True)
+    weights = [out_weight, shift(out_weight, "y", 4, 1), across, shift(out_weight, "y", 4, 3)]
 
     half = jax.ShapeDtypeStruct((4, 4 * rows, columns), F32)
     keep, give = local_call(

time: 128 us -> 126 us (0.984)
  starting transfers between devices: 46.1 us -> 44.8 us
    ppermute x26, waiting for transfers between devices: 31.7 us -> 43.4 us  [shift(): return lax.ppermute(x, axis, [(i, (i + step) % size) for i in range(size)])]
    all_to_all x1, waiting for transfers between devices: 13.3 us -> 2.03 us  [per_device(): attn = lax.all_to_all(attn, 'z', 0, 0, tiled=True)]
  transfers between devices with their start and end apart: 29 -> 29, of which waited for: 17 -> 20; matrix products, arithmetic and copies ran while one was open for 0% -> 0% of each run, Pallas kernels for 11% -> 12%
where the time goes in v3:
time: 126 us
  waiting for transfers between devices  54.2 us (43%)
  starting transfers between devices  44.8 us (36%)
  Pallas kernels  20.7 us (16%)
  local copies, waits for them, and re-layouts  4.78 us (4%)
    ppermute x26, waiting for transfers between devices, shift(): return lax.ppermute(x, axis, [(i, (i + step) % size) for i in range(size)])  43.4 us
    ppermute x26, starting transfers between devices, shift(): return lax.ppermute(x, axis, [(i, (i + step) % size) for i in range(size)])  35.3 us
    pallas_call x9, Pallas kernels, local_call(): pl.pallas_call(kernel, out_shape=out_shape, in_specs=[pl.BlockSpec(memory...  20.7 us
    ppermute x1, waiting for transfers between devices, per_device(): return lax.ppermute(total.astype(BF16), ('x', 'y'), swap)  5.58 us
    unnamed x10, local copies, waits for them, and re-layouts  4.67 us
    all_to_all x1, starting transfers between devices, per_device(): attn = lax.all_to_all(attn, 'z', 0, 0, tiled=True)  3.9 us
    all_to_all x1, starting transfers between devices, per_device(): got = lax.all_to_all(joined, 'z', 0, 0, tiled=True)  3.54 us
    all_to_all x1, waiting for transfers between devices, per_device(): got = lax.all_to_all(joined, 'z', 0, 0, tiled=True)  3.16 us
  transfers between devices with their start and end apart: 29, of which 20 were waited for; matrix products, arithmetic and copies ran while one was open for 0% of the time, Pallas kernels for 12%

profile of v3, /device:TPU:6, one launch (start us, length us, event | category | flops | bytes accessed | tf_op | source)
XLA Modules:
  0.0 125.6 jit_solution(7213457617180499286)
XLA Ops:
  1.8 3.1 %collective-permute-start.2 = (bf16[32,1152]{1,0:T(8,128)(2,1)S(1)}, bf16[32,1152]{1,0:T(8,128)(2,1)S(1)}, u32[]{:S(2)}, u32[]{:S(2)}) collective-permute-start(bf16[32,1152]{1,0:T(8,128)(2,1)S(1)} %concatenate.3), channel_id=1, source_target_pairs={{0,24},{8,0},{16,8},{24,16},{1,25},{9,1},{17,9},{25,17},{2,26},{10... | collective-permute-start | bytes 221192 | tf_op jit(solution)/shard_map/ppermute | solution.py:24
  7.3 3.6 %collective-permute-done.1 = bf16[32,1152]{1,0:T(8,128)(2,1)S(1)} collective-permute-done((bf16[32,1152]{1,0:T(8,128)(2,1)S(1)}, bf16[32,1152]{1,0:T(8,128)(2,1)S(1)}, u32[]{:S(2)}, u32[]{:S(2)}) %collective-permute-start.1) | collective-permute-done | bytes 73760 | tf_op jit(solution)/shard_map/ppermute | solution.py:24
  11.7 5.9 %collective-permute-start.4 = (bf16[4,32,1152]{2,1,0:T(8,128)(2,1)S(1)}, bf16[4,32,1152]{2,1,0:T(8,128)(2,1)S(1)}, u32[]{:S(2)}, u32[]{:S(2)}) collective-permute-start(bf16[4,32,1152]{2,1,0:T(8,128)(2,1)S(1)} %pad_maximum_fusion.refs_0_), channel_id=1, source_target_pairs={{0,7},{1,0},{2,1},{3,2},{4,3},{5,4},{6,5},{7,6},{8,15},{9,8},{10,9... | collective-permute-start | bytes 884744 | tf_op jit(solution)/shard_map/ppermute | solution.py:24
  20.8 2.0 %attend.5 = (f32[1,32,1152]{2,1,0:T(8,128)S(1)}, bf16[1,32,1152]{2,1,0:T(8,128)(2,1)S(1)}, bf16[1,32,1152]{2,1,0:T(8,128)(2,1)S(1)}, bf16[1,32,1152]{2,1,0:T(8,128)(2,1)S(1)}) custom-call(s32[1]{0:T(128)} %bitcast.3.me_ref, bf16[4,32,1152]{2,1,0:T(8,128)(2,1)S(1)} %pad_maximum_fusion.refs_0_, bf16[16,512,128]{2,1,0:T(8,128)(2,1)S(1)} %bitcast.31, ...), custom_call_target="tpu_custom_call" | custom-call | flops 536870912 | bytes 4857856 | tf_op jit(solution)/shard_map/attend/pallas_call | solution.py:133
  22.9 3.2 %collective-permute-done.3.refs_0_ = bf16[4,32,1152]{2,1,0:T(8,128)(2,1)S(1)} collective-permute-done((bf16[4,32,1152]{2,1,0:T(8,128)(2,1)S(1)}, bf16[4,32,1152]{2,1,0:T(8,128)(2,1)S(1)}, u32[]{:S(2)}, u32[]{:S(2)}) %collective-permute-start.3) | collective-permute-done | bytes 294944 | tf_op jit(solution)/shard_map/ppermute | solution.py:24
  26.1 3.2 %collective-permute-start.6 = (bf16[4,32,1152]{2,1,0:T(8,128)(2,1)S(1)}, bf16[4,32,1152]{2,1,0:T(8,128)(2,1)S(1)}, u32[]{:S(2)}, u32[]{:S(2)}) collective-permute-start(bf16[4,32,1152]{2,1,0:T(8,128)(2,1)S(1)} %collective-permute-done.4.refs_1_), channel_id=1, source_target_pairs={{0,7},{1,0},{2,1},{3,2},{4,3},{5,4},{6,5},{7,6},{8,15},{9,8},{10,9... | collective-permute-start | bytes 884744 | tf_op jit(solution)/shard_map/ppermute | solution.py:24
  29.4 3.5 %attend.6 = (f32[3,32,1152]{2,1,0:T(8,128)S(1)}, bf16[3,32,1152]{2,1,0:T(8,128)(2,1)S(1)}, bf16[3,32,1152]{2,1,0:T(8,128)(2,1)S(1)}, bf16[3,32,1152]{2,1,0:T(8,128)(2,1)S(1)}) custom-call(s32[1]{0:T(128)} %bitcast.3.me_ref, bf16[4,32,1152]{2,1,0:T(8,128)(2,1)S(1)} %collective-permute-done.3.refs_0_, bf16[4,32,1152]{2,1,0:T(8,128)(2,1)S(1)} %collective-permute-done.4.refs_1_, ...), custom_call_target="tpu_custom_call" | custom-call | flops 1073741824 | bytes 6258688 | tf_op jit(solution)/shard_map/attend/pallas_call | solution.py:133
  34.1 3.3 %collective-permute-start.8 = (bf16[4,32,1152]{2,1,0:T(8,128)(2,1)S(1)}, bf16[4,32,1152]{2,1,0:T(8,128)(2,1)S(1)}, u32[]{:S(2)}, u32[]{:S(2)}) collective-permute-start(bf16[4,32,1152]{2,1,0:T(8,128)(2,1)S(1)} %collective-permute-done.6.refs_1_), channel_id=1, source_target_pairs={{0,7},{1,0},{2,1},{3,2},{4,3},{5,4},{6,5},{7,6},{8,15},{9,8},{10,9... | collective-permute-start | bytes 884744 | tf_op jit(solution)/shard_map/ppermute | solution.py:24
  40.1 3.5 %attend.7 = (f32[2,32,1152]{2,1,0:T(8,128)S(1)}, bf16[2,32,1152]{2,1,0:T(8,128)(2,1)S(1)}, bf16[2,32,1152]{2,1,0:T(8,128)(2,1)S(1)}, bf16[2,32,1152]{2,1,0:T(8,128)(2,1)S(1)}) custom-call(s32[1]{0:T(128)} %bitcast.3.me_ref, bf16[4,32,1152]{2,1,0:T(8,128)(2,1)S(1)} %collective-permute-done.5.refs_0_, bf16[4,32,1152]{2,1,0:T(8,128)(2,1)S(1)} %collective-permute-done.6.refs_1_, ...), custom_call_target="tpu_custom_call" | custom-call | flops 1073741824 | bytes 5521408 | tf_op jit(solution)/shard_map/attend/pallas_call | solution.py:133
  43.7 2.1 %collective-permute-start.13 = (bf16[2,32,1152]{2,1,0:T(8,128)(2,1)S(1)}, bf16[2,32,1152]{2,1,0:T(8,128)(2,1)S(1)}, u32[]{:S(2)}, u32[]{:S(2)}) collective-permute-start(bf16[2,32,1152]{2,1,0:T(8,128)(2,1)S(1)} %get-tuple-element.102), channel_id=1, source_target_pairs={{0,24},{8,0},{16,8},{24,16},{1,25},{9,1},{17,9},{25,17},{2,26},{10... | collective-permute-start | bytes 442376 | tf_op jit(solution)/shard_map/ppermute | solution.py:24
  50.9 3.5 %attend.8 = (f32[2,32,1152]{2,1,0:T(8,128)S(1)}, bf16[2,32,1152]{2,1,0:T(8,128)(2,1)S(1)}, bf16[2,32,1152]{2,1,0:T(8,128)(2,1)S(1)}, bf16[2,32,1152]{2,1,0:T(8,128)(2,1)S(1)}) custom-call(s32[1]{0:T(128)} %bitcast.3.me_ref, bf16[4,32,1152]{2,1,0:T(8,128)(2,1)S(1)} %collective-permute-done.7.refs_0_, bf16[4,32,1152]{2,1,0:T(8,128)(2,1)S(1)} %collective-permute-done.8.refs_1_, ...), custom_call_target="tpu_custom_call" | custom-call | flops 1073741824 | bytes 5521408 | tf_op jit(solution)/shard_map/attend/pallas_call | solution.py:133
  54.8 2.1 %attend.9 = (f32[3,32,1152]{2,1,0:T(8,128)S(1)}, bf16[3,32,1152]{2,1,0:T(8,128)(2,1)S(1)}, bf16[3,32,1152]{2,1,0:T(8,128)(2,1)S(1)}, bf16[3,32,1152]{2,1,0:T(8,128)(2,1)S(1)}) custom-call(s32[1]{0:T(128)} %bitcast.3.me_ref, bf16[4,32,1152]{2,1,0:T(8,128)(2,1)S(1)} %collective-permute-done.9.refs_0_, bf16[16,512,128]{2,1,0:T(8,128)(2,1)S(1)} %bitcast.35, ...), custom_call_target="tpu_custom_call" | custom-call | flops 536870912 | bytes 6332416 | tf_op jit(solution)/shard_map/attend/pallas_call | solution.py:133
  56.9 2.1 %collective-permute-start.16 = (bf16[3,32,1152]{2,1,0:T(8,128)(2,1)S(1)}, bf16[3,32,1152]{2,1,0:T(8,128)(2,1)S(1)}, u32[]{:S(2)}, u32[]{:S(2)}) collective-permute-start(bf16[3,32,1152]{2,1,0:T(8,128)(2,1)S(1)} %get-tuple-element.111), channel_id=1, source_target_pairs={{0,24},{8,0},{16,8},{24,16},{1,25},{9,1},{17,9},{25,17},{2,26},{10... | collective-permute-start | bytes 663560 | tf_op jit(solution)/shard_map/ppermute | solution.py:24
  62.2 2.6 %collective-permute-done.16.refs_1_ = bf16[3,32,1152]{2,1,0:T(8,128)(2,1)S(1)} collective-permute-done((bf16[3,32,1152]{2,1,0:T(8,128)(2,1)S(1)}, bf16[3,32,1152]{2,1,0:T(8,128)(2,1)S(1)}, u32[]{:S(2)}, u32[]{:S(2)}) %collective-permute-start.16) | collective-permute-done | bytes 221216 | tf_op jit(solution)/shard_map/ppermute | solution.py:24
  70.4 3.5 %all-to-all-start = ((bf16[8,32,1152]{2,1,0:T(8,128)(2,1)}), bf16[8,32,1152]{2,1,0:T(8,128)(2,1)S(1)}, u32[]{:S(2)}, u32[]{:S(2)}) async-start(bf16[8,32,1152]{2,1,0:T(8,128)(2,1)} %get-tuple-element.125), calls=%async_computation | async-start | bytes 1179648 | tf_op jit(solution)/shard_map/all_to_all | solution.py:278
  74.8 10.0 %collective-permute-done.19.refs_2_ = bf16[1024,256]{1,0:T(8,128)(2,1)S(1)} collective-permute-done((bf16[1024,256]{1,0:T(8,128)(2,1)S(1)}, bf16[1024,256]{1,0:T(8,128)(2,1)S(1)}, u32[]{:S(2)}, u32[]{:S(2)}) %collective-permute-start.19) | collective-permute-done | bytes 524320 | tf_op jit(solution)/shard_map/ppermute | solution.py:24
  84.8 3.2 %all-to-all-done.got_ref = bf16[8,32,1152]{2,1,0:T(8,128)(2,1)S(1)} async-done(((bf16[8,32,1152]{2,1,0:T(8,128)(2,1)}), bf16[8,32,1152]{2,1,0:T(8,128)(2,1)S(1)}, u32[]{:S(2)}, u32[]{:S(2)}) %all-to-all-start) | async-done | bytes 589856 | tf_op jit(solution)/shard_map/all_to_all | solution.py:278
  89.3 3.9 %all-to-all-start.1 = ((bf16[8,32,1024]{2,1,0:T(8,128)(2,1)}), bf16[8,32,1024]{2,1,0:T(8,128)(2,1)S(1)}, u32[]{:S(2)}, u32[]{:S(2)}) async-start(bf16[8,32,1024]{2,1,0:T(8,128)(2,1)} %finish.1), calls=%async_computation.1 | async-start | bytes 1048576 | tf_op jit(solution)/shard_map/all_to_all | solution.py:284
  95.3 7.2 %collective-permute-done.21.refs_3_ = bf16[1024,256]{1,0:T(8,128)(2,1)S(1)} collective-permute-done((bf16[1024,256]{1,0:T(8,128)(2,1)S(1)}, bf16[1024,256]{1,0:T(8,128)(2,1)S(1)}, u32[]{:S(2)}, u32[]{:S(2)}) %collective-permute-start.21) | collective-permute-done | bytes 524320 | tf_op jit(solution)/shard_map/ppermute | solution.py:24
  102.4 2.1 %collective-permute-done.20.refs_1_ = bf16[1024,256]{1,0:T(8,128)(2,1)S(1)} collective-permute-done((bf16[1024,256]{1,0:T(8,128)(2,1)S(1)}, bf16[1024,256]{1,0:T(8,128)(2,1)S(1)}, u32[]{:S(2)}, u32[]{:S(2)}) %collective-permute-start.20) | collective-permute-done | bytes 524320 | tf_op jit(solution)/shard_map/ppermute | solution.py:24
  104.5 2.0 %all-to-all-done.1.attn_ref = bf16[8,32,1024]{2,1,0:T(8,128)(2,1)S(1)} async-done(((bf16[8,32,1024]{2,1,0:T(8,128)(2,1)}), bf16[8,32,1024]{2,1,0:T(8,128)(2,1)S(1)}, u32[]{:S(2)}, u32[]{:S(2)}) %all-to-all-start.1) | async-done | bytes 524320 | tf_op jit(solution)/shard_map/all_to_all | solution.py:284
  113.7 2.4 %collective-permute-done.25 = bf16[128,256]{1,0:T(8,128)(2,1)S(1)} collective-permute-done((bf16[128,256]{1,0:T(8,128)(2,1)S(1)}, bf16[128,256]{1,0:T(8,128)(2,1)S(1)}, u32[]{:S(2)}, u32[]{:S(2)}) %collective-permute-start.25) | collective-permute-done | bytes 65568 | tf_op jit(solution)/shard_map/ppermute | solution.py:24
  117.3 2.1 %collective-permute-start.26 = (bf16[128,256]{1,0:T(8,128)(2,1)S(1)}, bf16[128,256]{1,0:T(8,128)(2,1)S(1)}, u32[]{:S(2)}, u32[]{:S(2)}) collective-permute-start(bf16[128,256]{1,0:T(8,128)(2,1)S(1)} %fusion.3), channel_id=1, source_target_pairs={{128,0},{192,24},{0,16},{64,8},{200,72},{8,64},{72,88},{136,80},{1... | collective-permute-start | bytes 196616 | tf_op jit(solution)/shard_map/ppermute | solution.py:303
  119.4 5.6 %collective-permute-done.26 = bf16[128,256]{1,0:T(8,128)(2,1)S(1)} collective-permute-done((bf16[128,256]{1,0:T(8,128)(2,1)S(1)}, bf16[128,256]{1,0:T(8,128)(2,1)S(1)}, u32[]{:S(2)}, u32[]{:S(2)}) %collective-permute-start.26) | collective-permute-done | bytes 65568 | tf_op jit(solution)/shard_map/ppermute | solution.py:303
  (60 shorter events, 39.6 us)
Async XLA Ops:
  5.5 6.2 %collective-permute-start = (bf16[32,1152]{1,0:T(8,128)(2,1)S(1)}, bf16[32,1152]{1,0:T(8,128)(2,1)S(1)}, u32[]{:S(2)}, u32[]{:S(2)}) collective-permute-start(bf16[32,1152]{1,0:T(8,128)(2,1)S(1)} %concatenate.3), channel_id=1, source_target_pairs={{0,8},{8,16},{16,24},{24,0},{1,9},{9,17},{17,25},{25,1},{2,10},{10... | collective-permute-start | bytes 221192 | tf_op jit(solution)/shard_map/ppermute | solution.py:24
  11.7 11.2 %collective-permute-start.4 = (bf16[4,32,1152]{2,1,0:T(8,128)(2,1)S(1)}, bf16[4,32,1152]{2,1,0:T(8,128)(2,1)S(1)}, u32[]{:S(2)}, u32[]{:S(2)}) collective-permute-start(bf16[4,32,1152]{2,1,0:T(8,128)(2,1)S(1)} %pad_maximum_fusion.refs_0_), channel_id=1, source_target_pairs={{0,7},{1,0},{2,1},{3,2},{4,3},{5,4},{6,5},{7,6},{8,15},{9,8},{10,9... | collective-permute-start | bytes 884744 | tf_op jit(solution)/shard_map/ppermute | solution.py:24
  17.6 8.5 %collective-permute-start.3 = (bf16[4,32,1152]{2,1,0:T(8,128)(2,1)S(1)}, bf16[4,32,1152]{2,1,0:T(8,128)(2,1)S(1)}, u32[]{:S(2)}, u32[]{:S(2)}) collective-permute-start(bf16[4,32,1152]{2,1,0:T(8,128)(2,1)S(1)} %pad_maximum_fusion.refs_0_), channel_id=1, source_target_pairs={{0,1},{1,2},{2,3},{3,4},{4,5},{5,6},{6,7},{7,0},{8,9},{9,10},{10,1... | collective-permute-start | bytes 884744 | tf_op jit(solution)/shard_map/ppermute | solution.py:24
  26.1 7.9 %collective-permute-start.5 = (bf16[4,32,1152]{2,1,0:T(8,128)(2,1)S(1)}, bf16[4,32,1152]{2,1,0:T(8,128)(2,1)S(1)}, u32[]{:S(2)}, u32[]{:S(2)}) collective-permute-start(bf16[4,32,1152]{2,1,0:T(8,128)(2,1)S(1)} %collective-permute-done.3.refs_0_), channel_id=1, source_target_pairs={{0,1},{1,2},{2,3},{3,4},{4,5},{5,6},{6,7},{7,0},{8,9},{9,10},{10,1... | collective-permute-start | bytes 884744 | tf_op jit(solution)/shard_map/ppermute | solution.py:24
  26.1 7.9 %collective-permute-start.6 = (bf16[4,32,1152]{2,1,0:T(8,128)(2,1)S(1)}, bf16[4,32,1152]{2,1,0:T(8,128)(2,1)S(1)}, u32[]{:S(2)}, u32[]{:S(2)}) collective-permute-start(bf16[4,32,1152]{2,1,0:T(8,128)(2,1)S(1)} %collective-permute-done.4.refs_1_), channel_id=1, source_target_pairs={{0,7},{1,0},{2,1},{3,2},{4,3},{5,4},{6,5},{7,6},{8,15},{9,8},{10,9... | collective-permute-start | bytes 884744 | tf_op jit(solution)/shard_map/ppermute | solution.py:24
  34.1 9.5 %collective-permute-start.7 = (bf16[4,32,1152]{2,1,0:T(8,128)(2,1)S(1)}, bf16[4,32,1152]{2,1,0:T(8,128)(2,1)S(1)}, u32[]{:S(2)}, u32[]{:S(2)}) collective-permute-start(bf16[4,32,1152]{2,1,0:T(8,128)(2,1)S(1)} %collective-permute-done.5.refs_0_), channel_id=1, source_target_pairs={{0,1},{1,2},{2,3},{3,4},{4,5},{5,6},{6,7},{7,0},{8,9},{9,10},{10,1... | collective-permute-start | bytes 884744 | tf_op jit(solution)/shard_map/ppermute | solution.py:24
  34.1 9.5 %collective-permute-start.8 = (bf16[4,32,1152]{2,1,0:T(8,128)(2,1)S(1)}, bf16[4,32,1152]{2,1,0:T(8,128)(2,1)S(1)}, u32[]{:S(2)}, u32[]{:S(2)}) collective-permute-start(bf16[4,32,1152]{2,1,0:T(8,128)(2,1)S(1)} %collective-permute-done.6.refs_1_), channel_id=1, source_target_pairs={{0,7},{1,0},{2,1},{3,2},{4,3},{5,4},{6,5},{7,6},{8,15},{9,8},{10,9... | collective-permute-start | bytes 884744 | tf_op jit(solution)/shard_map/ppermute | solution.py:24
  37.4 8.4 %collective-permute-start.10 = (bf16[3,32,1152]{2,1,0:T(8,128)(2,1)S(1)}, bf16[3,32,1152]{2,1,0:T(8,128)(2,1)S(1)}, u32[]{:S(2)}, u32[]{:S(2)}) collective-permute-start(bf16[3,32,1152]{2,1,0:T(8,128)(2,1)S(1)} %get-tuple-element.92), channel_id=1, source_target_pairs={{0,24},{8,0},{16,8},{24,16},{1,25},{9,1},{17,9},{25,17},{2,26},{10... | collective-permute-start | bytes 663560 | tf_op jit(solution)/shard_map/ppermute | solution.py:24
  38.0 9.4 %collective-permute-start.11 = (bf16[3,32,1152]{2,1,0:T(8,128)(2,1)S(1)}, bf16[3,32,1152]{2,1,0:T(8,128)(2,1)S(1)}, u32[]{:S(2)}, u32[]{:S(2)}) collective-permute-start(bf16[3,32,1152]{2,1,0:T(8,128)(2,1)S(1)} %get-tuple-element.93), channel_id=1, source_target_pairs={{0,16},{8,24},{16,0},{24,8},{1,17},{9,25},{17,1},{25,9},{2,18},{10... | collective-permute-start | bytes 663560 | tf_op jit(solution)/shard_map/ppermute | solution.py:24
  38.6 12.3 %collective-permute-start.12 = (bf16[3,32,1152]{2,1,0:T(8,128)(2,1)S(1)}, bf16[3,32,1152]{2,1,0:T(8,128)(2,1)S(1)}, u32[]{:S(2)}, u32[]{:S(2)}) collective-permute-start(bf16[3,32,1152]{2,1,0:T(8,128)(2,1)S(1)} %get-tuple-element.94), channel_id=1, source_target_pairs={{0,8},{8,16},{16,24},{24,0},{1,9},{9,17},{17,25},{25,1},{2,10},{10... | collective-permute-start | bytes 663560 | tf_op jit(solution)/shard_map/ppermute | solution.py:24
  43.6 11.2 %collective-permute-start.9 = (bf16[4,32,1152]{2,1,0:T(8,128)(2,1)S(1)}, bf16[4,32,1152]{2,1,0:T(8,128)(2,1)S(1)}, u32[]{:S(2)}, u32[]{:S(2)}) collective-permute-start(bf16[4,32,1152]{2,1,0:T(8,128)(2,1)S(1)} %collective-permute-done.7.refs_0_), channel_id=1, source_target_pairs={{0,1},{1,2},{2,3},{3,4},{4,5},{5,6},{6,7},{7,0},{8,9},{9,10},{10,1... | collective-permute-start | bytes 884744 | tf_op jit(solution)/shard_map/ppermute | solution.py:24
  43.7 10.8 %collective-permute-start.13 = (bf16[2,32,1152]{2,1,0:T(8,128)(2,1)S(1)}, bf16[2,32,1152]{2,1,0:T(8,128)(2,1)S(1)}, u32[]{:S(2)}, u32[]{:S(2)}) collective-permute-start(bf16[2,32,1152]{2,1,0:T(8,128)(2,1)S(1)} %get-tuple-element.102), channel_id=1, source_target_pairs={{0,24},{8,0},{16,8},{24,16},{1,25},{9,1},{17,9},{25,17},{2,26},{10... | collective-permute-start | bytes 442376 | tf_op jit(solution)/shard_map/ppermute | solution.py:24
  45.8 8.7 %collective-permute-start.14 = (bf16[2,32,1152]{2,1,0:T(8,128)(2,1)S(1)}, bf16[2,32,1152]{2,1,0:T(8,128)(2,1)S(1)}, u32[]{:S(2)}, u32[]{:S(2)}) collective-permute-start(bf16[2,32,1152]{2,1,0:T(8,128)(2,1)S(1)} %get-tuple-element.103), channel_id=1, source_target_pairs={{0,16},{8,24},{16,0},{24,8},{1,17},{9,25},{17,1},{25,9},{2,18},{10... | collective-permute-start | bytes 442376 | tf_op jit(solution)/shard_map/ppermute | solution.py:24
  47.4 7.4 %collective-permute-start.15 = (bf16[2,32,1152]{2,1,0:T(8,128)(2,1)S(1)}, bf16[2,32,1152]{2,1,0:T(8,128)(2,1)S(1)}, u32[]{:S(2)}, u32[]{:S(2)}) collective-permute-start(bf16[2,32,1152]{2,1,0:T(8,128)(2,1)S(1)} %get-tuple-element.104), channel_id=1, source_target_pairs={{0,8},{8,16},{16,24},{24,0},{1,9},{9,17},{17,25},{25,1},{2,10},{10... | collective-permute-start | bytes 442376 | tf_op jit(solution)/shard_map/ppermute | solution.py:24
  56.9 8.0 %collective-permute-start.16 = (bf16[3,32,1152]{2,1,0:T(8,128)(2,1)S(1)}, bf16[3,32,1152]{2,1,0:T(8,128)(2,1)S(1)}, u32[]{:S(2)}, u32[]{:S(2)}) collective-permute-start(bf16[3,32,1152]{2,1,0:T(8,128)(2,1)S(1)} %get-tuple-element.111), channel_id=1, source_target_pairs={{0,24},{8,0},{16,8},{24,16},{1,25},{9,1},{17,9},{25,17},{2,26},{10... | collective-permute-start | bytes 663560 | tf_op jit(solution)/shard_map/ppermute | solution.py:24
  59.0 7.5 %collective-permute-start.17 = (bf16[3,32,1152]{2,1,0:T(8,128)(2,1)S(1)}, bf16[3,32,1152]{2,1,0:T(8,128)(2,1)S(1)}, u32[]{:S(2)}, u32[]{:S(2)}) collective-permute-start(bf16[3,32,1152]{2,1,0:T(8,128)(2,1)S(1)} %get-tuple-element.112), channel_id=1, source_target_pairs={{0,16},{8,24},{16,0},{24,8},{1,17},{9,25},{17,1},{25,9},{2,18},{10... | collective-permute-start | bytes 663560 | tf_op jit(solution)/shard_map/ppermute | solution.py:24
  59.0 9.5 %collective-permute-start.18 = (bf16[3,32,1152]{2,1,0:T(8,128)(2,1)S(1)}, bf16[3,32,1152]{2,1,0:T(8,128)(2,1)S(1)}, u32[]{:S(2)}, u32[]{:S(2)}) collective-permute-start(bf16[3,32,1152]{2,1,0:T(8,128)(2,1)S(1)} %get-tuple-element.113), channel_id=1, source_target_pairs={{0,8},{8,16},{16,24},{24,0},{1,9},{9,17},{17,25},{25,1},{2,10},{10... | collective-permute-start | bytes 663560 | tf_op jit(solution)/shard_map/ppermute | solution.py:24
  70.4 17.5 %all-to-all-start = ((bf16[8,32,1152]{2,1,0:T(8,128)(2,1)}), bf16[8,32,1152]{2,1,0:T(8,128)(2,1)S(1)}, u32[]{:S(2)}, u32[]{:S(2)}) async-start(bf16[8,32,1152]{2,1,0:T(8,128)(2,1)} %get-tuple-element.125), calls=%async_computation | async-start | bytes 1179648 | tf_op jit(solution)/shard_map/all_to_all | solution.py:278
  74.0 10.8 %collective-permute-start.19 = (bf16[1024,256]{1,0:T(8,128)(2,1)S(1)}, bf16[1024,256]{1,0:T(8,128)(2,1)S(1)}, u32[]{:S(2)}, u32[]{:S(2)}) collective-permute-start(bf16[1024,256]{1,0:T(8,128)(2,1)S(1)} %copy-done.3), channel_id=1, source_target_pairs={{0,16},{8,24},{16,0},{24,8},{1,17},{9,25},{17,1},{25,9},{2,18},{10... | collective-permute-start | bytes 1572872 | tf_op jit(solution)/shard_map/ppermute | solution.py:24
  89.3 17.2 %all-to-all-start.1 = ((bf16[8,32,1024]{2,1,0:T(8,128)(2,1)}), bf16[8,32,1024]{2,1,0:T(8,128)(2,1)S(1)}, u32[]{:S(2)}, u32[]{:S(2)}) async-start(bf16[8,32,1024]{2,1,0:T(8,128)(2,1)} %finish.1), calls=%async_computation.1 | async-start | bytes 1048576 | tf_op jit(solution)/shard_map/all_to_all | solution.py:284
  93.2 9.2 %collective-permute-start.21 = (bf16[1024,256]{1,0:T(8,128)(2,1)S(1)}, bf16[1024,256]{1,0:T(8,128)(2,1)S(1)}, u32[]{:S(2)}, u32[]{:S(2)}) collective-permute-start(bf16[1024,256]{1,0:T(8,128)(2,1)S(1)} %copy-done.3), channel_id=1, source_target_pairs={{0,24},{8,0},{16,8},{24,16},{1,25},{9,1},{17,9},{25,17},{2,26},{10... | collective-permute-start | bytes 1572872 | tf_op jit(solution)/shard_map/ppermute | solution.py:24
  94.1 10.4 %collective-permute-start.20 = (bf16[1024,256]{1,0:T(8,128)(2,1)S(1)}, bf16[1024,256]{1,0:T(8,128)(2,1)S(1)}, u32[]{:S(2)}, u32[]{:S(2)}) collective-permute-start(bf16[1024,256]{1,0:T(8,128)(2,1)S(1)} %copy-done.3), channel_id=1, source_target_pairs={{0,8},{8,16},{16,24},{24,0},{1,9},{9,17},{17,25},{25,1},{2,10},{10... | collective-permute-start | bytes 1572872 | tf_op jit(solution)/shard_map/ppermute | solution.py:24
  109.9 6.2 %collective-permute-start.25 = (bf16[128,256]{1,0:T(8,128)(2,1)S(1)}, bf16[128,256]{1,0:T(8,128)(2,1)S(1)}, u32[]{:S(2)}, u32[]{:S(2)}) collective-permute-start(bf16[128,256]{1,0:T(8,128)(2,1)S(1)} %get-tuple-element.136), channel_id=1, source_target_pairs={{0,192},{64,0},{128,64},{192,128},{1,193},{65,1},{129,65},{193,129... | collective-permute-start | bytes 196616 | tf_op jit(solution)/shard_map/ppermute | solution.py:24
  117.3 7.7 %collective-permute-start.26 = (bf16[128,256]{1,0:T(8,128)(2,1)S(1)}, bf16[128,256]{1,0:T(8,128)(2,1)S(1)}, u32[]{:S(2)}, u32[]{:S(2)}) collective-permute-start(bf16[128,256]{1,0:T(8,128)(2,1)S(1)} %fusion.3), channel_id=1, source_target_pairs={{128,0},{192,24},{0,16},{64,8},{200,72},{8,64},{72,88},{136,80},{1... | collective-permute-start | bytes 196616 | tf_op jit(solution)/shard_map/ppermute | solution.py:303
  (9 other events, 57.5 us)

commit v4 on v3

--- a/solution.py
+++ b/solution.py
@@ -255,18 +255,19 @@
     low_1, high_1, near = tie((low_1, high_1, near))
     low_2, high_2 = shift(low_1, "z", 8, 1), shift(high_1, "z", 8, -1)
     near = attend(me, [low_1, high_1], keys, values, near)
+    across = shift(out_weight, "y", 4, 2)
     low_2, high_2, near = tie((low_2, high_2, near))
     low_3, high_3 = shift(low_2, "z", 8, 1), shift(high_2, "z", 8, -1)
     near = send(near)
     second = attend(me, [low_2, high_2], keys, values)
-    low_3, high_3, second = tie((low_3, high_3, second))
+    low_3, high_3, second, across, out_weight = tie((low_3, high_3, second, across, out_weight))
     far = shift(low_3, "z", 8, 1)
     second = send(second)
     low_3, high_3, near = tie((low_3, high_3, near))
     third = attend(me, [low_3, high_3], keys, values)
     far, third, second, out_weight = tie((far, third, second, out_weight))
     third = send(attend(me, [far], keys, values, third))
-    across = shift(out_weight, "y", 4, 2)
+    beside = [shift(out_weight, "y", 4, step) for step in (1, 3)]
 
     line = [jax.ShapeDtypeStruct((8, rows, WIDE), BF16), jax.ShapeDtypeStruct((rows, WIDE), F32)]
     joined = local_call(
@@ -276,13 +277,12 @@
         functools.partial(line_kernel, [3], 5), "line", [my_z], [*third, *joined], line
     )
     got = lax.all_to_all(joined, "z", 0, 0, tiled=True)
-    got, across = tie((got, across))
     (attn,) = local_call(
         finish_kernel, "finish", [my_z], [mine, got], [jax.ShapeDtypeStruct((8, rows, FLAT), BF16)]
     )
-    attn, out_weight = tie((attn, out_weight))
+    attn, beside = tie((attn, beside))
     attn = lax.all_to_all(attn, "z", 0, 0, tiled=True)
-    weights = [out_weight, shift(out_weight, "y", 4, 1), across, shift(out_weight, "y", 4, 3)]
+    weights = [out_weight, beside[0], across, beside[1]]
 
     half = jax.ShapeDtypeStruct((4, 4 * rows, columns), F32)
     keep, give = local_call(

time: 126 us -> 125 us (level)
    ppermute x26, waiting for transfers between devices: 43.4 us -> 23.1 us  [shift(): return lax.ppermute(x, axis, [(i, (i + step) % size) for i in range(size)])]
    all_to_all x1, waiting for transfers between devices: 2.03 us -> 12.9 us  [per_device(): attn = lax.all_to_all(attn, 'z', 0, 0, tiled=True)]
    all_to_all x1, waiting for transfers between devices: 3.16 us -> 11.8 us  [per_device(): got = lax.all_to_all(joined, 'z', 0, 0, tiled=True)]
  transfers between devices with their start and end apart: 29 -> 29, of which waited for: 20 -> 17; matrix products, arithmetic and copies ran while one was open for 0% -> 0% of each run, Pallas kernels for 12% -> 13%
where the time goes in v4:
time: 125 us
  waiting for transfers between devices  53.4 us (43%)
  starting transfers between devices  45 us (36%)
  Pallas kernels  20.7 us (17%)
  local copies, waits for them, and re-layouts  4.78 us (4%)
    ppermute x26, starting transfers between devices, shift(): return lax.ppermute(x, axis, [(i, (i + step) % size) for i in range(size)])  35.6 us
    ppermute x26, waiting for transfers between devices, shift(): return lax.ppermute(x, axis, [(i, (i + step) % size) for i in range(size)])  23.1 us
    pallas_call x9, Pallas kernels, local_call(): pl.pallas_call(kernel, out_shape=out_shape, in_specs=[pl.BlockSpec(memory...  20.7 us
    all_to_all x1, waiting for transfers between devices, per_device(): attn = lax.all_to_all(attn, 'z', 0, 0, tiled=True)  12.9 us
    all_to_all x1, waiting for transfers between devices, per_device(): got = lax.all_to_all(joined, 'z', 0, 0, tiled=True)  11.8 us
    ppermute x1, waiting for transfers between devices, per_device(): return lax.ppermute(total.astype(BF16), ('x', 'y'), swap)  5.57 us
    unnamed x10, local copies, waits for them, and re-layouts  4.67 us
    all_to_all x1, starting transfers between devices, per_device(): attn = lax.all_to_all(attn, 'z', 0, 0, tiled=True)  3.75 us
  transfers between devices with their start and end apart: 29, of which 17 were waited for; matrix products, arithmetic and copies ran while one was open for 0% of the time, Pallas kernels for 13%

profile of v4, /device:TPU:6, one launch (start us, length us, event | category | flops | bytes accessed | tf_op | source)
XLA Modules:
  0.0 125.0 jit_solution(14070533627246243614)
XLA Ops:
  1.8 3.1 %collective-permute-start.2 = (bf16[32,1152]{1,0:T(8,128)(2,1)S(1)}, bf16[32,1152]{1,0:T(8,128)(2,1)S(1)}, u32[]{:S(2)}, u32[]{:S(2)}) collective-permute-start(bf16[32,1152]{1,0:T(8,128)(2,1)S(1)} %concatenate.3), channel_id=1, source_target_pairs={{0,24},{8,0},{16,8},{24,16},{1,25},{9,1},{17,9},{25,17},{2,26},{10... | collective-permute-start | bytes 221192 | tf_op jit(solution)/shard_map/ppermute | solution.py:24
  7.3 3.6 %collective-permute-done.1 = bf16[32,1152]{1,0:T(8,128)(2,1)S(1)} collective-permute-done((bf16[32,1152]{1,0:T(8,128)(2,1)S(1)}, bf16[32,1152]{1,0:T(8,128)(2,1)S(1)}, u32[]{:S(2)}, u32[]{:S(2)}) %collective-permute-start.1) | collective-permute-done | bytes 73760 | tf_op jit(solution)/shard_map/ppermute | solution.py:24
  11.7 5.9 %collective-permute-start.4 = (bf16[4,32,1152]{2,1,0:T(8,128)(2,1)S(1)}, bf16[4,32,1152]{2,1,0:T(8,128)(2,1)S(1)}, u32[]{:S(2)}, u32[]{:S(2)}) collective-permute-start(bf16[4,32,1152]{2,1,0:T(8,128)(2,1)S(1)} %pad_maximum_fusion.refs_0_), channel_id=1, source_target_pairs={{0,7},{1,0},{2,1},{3,2},{4,3},{5,4},{6,5},{7,6},{8,15},{9,8},{10,9... | collective-permute-start | bytes 884744 | tf_op jit(solution)/shard_map/ppermute | solution.py:24
  21.9 2.0 %attend.5 = (f32[1,32,1152]{2,1,0:T(8,128)S(1)}, bf16[1,32,1152]{2,1,0:T(8,128)(2,1)S(1)}, bf16[1,32,1152]{2,1,0:T(8,128)(2,1)S(1)}, bf16[1,32,1152]{2,1,0:T(8,128)(2,1)S(1)}) custom-call(s32[1]{0:T(128)} %bitcast.3.me_ref, bf16[4,32,1152]{2,1,0:T(8,128)(2,1)S(1)} %pad_maximum_fusion.refs_0_, bf16[16,512,128]{2,1,0:T(8,128)(2,1)S(1)} %bitcast.31, ...), custom_call_target="tpu_custom_call" | custom-call | flops 536870912 | bytes 4857856 | tf_op jit(solution)/shard_map/attend/pallas_call | solution.py:133
  23.9 2.2 %collective-permute-done.3.refs_0_ = bf16[4,32,1152]{2,1,0:T(8,128)(2,1)S(1)} collective-permute-done((bf16[4,32,1152]{2,1,0:T(8,128)(2,1)S(1)}, bf16[4,32,1152]{2,1,0:T(8,128)(2,1)S(1)}, u32[]{:S(2)}, u32[]{:S(2)}) %collective-permute-start.3) | collective-permute-done | bytes 294944 | tf_op jit(solution)/shard_map/ppermute | solution.py:24
  26.1 3.2 %collective-permute-start.6 = (bf16[4,32,1152]{2,1,0:T(8,128)(2,1)S(1)}, bf16[4,32,1152]{2,1,0:T(8,128)(2,1)S(1)}, u32[]{:S(2)}, u32[]{:S(2)}) collective-permute-start(bf16[4,32,1152]{2,1,0:T(8,128)(2,1)S(1)} %collective-permute-done.4.refs_1_), channel_id=1, source_target_pairs={{0,7},{1,0},{2,1},{3,2},{4,3},{5,4},{6,5},{7,6},{8,15},{9,8},{10,9... | collective-permute-start | bytes 884744 | tf_op jit(solution)/shard_map/ppermute | solution.py:24
  29.4 3.5 %attend.6 = (f32[3,32,1152]{2,1,0:T(8,128)S(1)}, bf16[3,32,1152]{2,1,0:T(8,128)(2,1)S(1)}, bf16[3,32,1152]{2,1,0:T(8,128)(2,1)S(1)}, bf16[3,32,1152]{2,1,0:T(8,128)(2,1)S(1)}) custom-call(s32[1]{0:T(128)} %bitcast.3.me_ref, bf16[4,32,1152]{2,1,0:T(8,128)(2,1)S(1)} %collective-permute-done.3.refs_0_, bf16[4,32,1152]{2,1,0:T(8,128)(2,1)S(1)} %collective-permute-done.4.refs_1_, ...), custom_call_target="tpu_custom_call" | custom-call | flops 1073741824 | bytes 6258688 | tf_op jit(solution)/shard_map/attend/pallas_call | solution.py:133
  34.1 3.2 %collective-permute-start.8 = (bf16[4,32,1152]{2,1,0:T(8,128)(2,1)S(1)}, bf16[4,32,1152]{2,1,0:T(8,128)(2,1)S(1)}, u32[]{:S(2)}, u32[]{:S(2)}) collective-permute-start(bf16[4,32,1152]{2,1,0:T(8,128)(2,1)S(1)} %collective-permute-done.6.refs_1_), channel_id=1, source_target_pairs={{0,7},{1,0},{2,1},{3,2},{4,3},{5,4},{6,5},{7,6},{8,15},{9,8},{10,9... | collective-permute-start | bytes 884744 | tf_op jit(solution)/shard_map/ppermute | solution.py:24
  40.1 3.5 %attend.7 = (f32[2,32,1152]{2,1,0:T(8,128)S(1)}, bf16[2,32,1152]{2,1,0:T(8,128)(2,1)S(1)}, bf16[2,32,1152]{2,1,0:T(8,128)(2,1)S(1)}, bf16[2,32,1152]{2,1,0:T(8,128)(2,1)S(1)}) custom-call(s32[1]{0:T(128)} %bitcast.3.me_ref, bf16[4,32,1152]{2,1,0:T(8,128)(2,1)S(1)} %collective-permute-done.5.refs_0_, bf16[4,32,1152]{2,1,0:T(8,128)(2,1)S(1)} %collective-permute-done.6.refs_1_, ...), custom_call_target="tpu_custom_call" | custom-call | flops 1073741824 | bytes 5521408 | tf_op jit(solution)/shard_map/attend/pallas_call | solution.py:133
  43.7 2.0 %collective-permute-start.14 = (bf16[2,32,1152]{2,1,0:T(8,128)(2,1)S(1)}, bf16[2,32,1152]{2,1,0:T(8,128)(2,1)S(1)}, u32[]{:S(2)}, u32[]{:S(2)}) collective-permute-start(bf16[2,32,1152]{2,1,0:T(8,128)(2,1)S(1)} %get-tuple-element.103), channel_id=1, source_target_pairs={{0,24},{8,0},{16,8},{24,16},{1,25},{9,1},{17,9},{25,17},{2,26},{10... | collective-permute-start | bytes 442376 | tf_op jit(solution)/shard_map/ppermute | solution.py:24
  50.8 3.5 %attend.8 = (f32[2,32,1152]{2,1,0:T(8,128)S(1)}, bf16[2,32,1152]{2,1,0:T(8,128)(2,1)S(1)}, bf16[2,32,1152]{2,1,0:T(8,128)(2,1)S(1)}, bf16[2,32,1152]{2,1,0:T(8,128)(2,1)S(1)}) custom-call(s32[1]{0:T(128)} %bitcast.3.me_ref, bf16[4,32,1152]{2,1,0:T(8,128)(2,1)S(1)} %collective-permute-done.7.refs_0_, bf16[4,32,1152]{2,1,0:T(8,128)(2,1)S(1)} %collective-permute-done.8.refs_1_, ...), custom_call_target="tpu_custom_call" | custom-call | flops 1073741824 | bytes 5521408 | tf_op jit(solution)/shard_map/attend/pallas_call | solution.py:133
  54.7 2.1 %attend.9 = (f32[3,32,1152]{2,1,0:T(8,128)S(1)}, bf16[3,32,1152]{2,1,0:T(8,128)(2,1)S(1)}, bf16[3,32,1152]{2,1,0:T(8,128)(2,1)S(1)}, bf16[3,32,1152]{2,1,0:T(8,128)(2,1)S(1)}) custom-call(s32[1]{0:T(128)} %bitcast.3.me_ref, bf16[4,32,1152]{2,1,0:T(8,128)(2,1)S(1)} %collective-permute-done.10.refs_0_, bf16[16,512,128]{2,1,0:T(8,128)(2,1)S(1)} %bitcast.35, ...), custom_call_target="tpu_custom_call" | custom-call | flops 536870912 | bytes 6332416 | tf_op jit(solution)/shard_map/attend/pallas_call | solution.py:133
  56.8 2.1 %collective-permute-start.17 = (bf16[3,32,1152]{2,1,0:T(8,128)(2,1)S(1)}, bf16[3,32,1152]{2,1,0:T(8,128)(2,1)S(1)}, u32[]{:S(2)}, u32[]{:S(2)}) collective-permute-start(bf16[3,32,1152]{2,1,0:T(8,128)(2,1)S(1)} %get-tuple-element.113), channel_id=1, source_target_pairs={{0,24},{8,0},{16,8},{24,16},{1,25},{9,1},{17,9},{25,17},{2,26},{10... | collective-permute-start | bytes 663560 | tf_op jit(solution)/shard_map/ppermute | solution.py:24
  60.2 1.9 %line.2 = (bf16[8,32,1152]{2,1,0:T(8,128)(2,1)S(1)}, f32[32,1152]{1,0:T(8,128)S(1)}) custom-call(s32[1]{0:T(128)} %bitcast.2.z_ref, f32[3,32,1152]{2,1,0:T(8,128)S(1)} %get-tuple-element.116.refs_0_, bf16[3,32,1152]{2,1,0:T(8,128)(2,1)S(1)} %collective-permute-done.11.refs_1_, bf16[3,32,1152]{2,1,0:T(8,128)(2,1)S(1)} %collective-permute-done.12.refs_2_, ...), custom_call_target="tpu_custom_call" | custom-call | bytes 2580480 | tf_op jit(solution)/shard_map/line/pallas_call | solution.py:133
  62.1 2.6 %collective-permute-done.17.refs_1_ = bf16[3,32,1152]{2,1,0:T(8,128)(2,1)S(1)} collective-permute-done((bf16[3,32,1152]{2,1,0:T(8,128)(2,1)S(1)}, bf16[3,32,1152]{2,1,0:T(8,128)(2,1)S(1)}, u32[]{:S(2)}, u32[]{:S(2)}) %collective-permute-start.17) | collective-permute-done | bytes 221216 | tf_op jit(solution)/shard_map/ppermute | solution.py:24
  66.4 2.0 %collective-permute-done.19.refs_3_ = bf16[3,32,1152]{2,1,0:T(8,128)(2,1)S(1)} collective-permute-done((bf16[3,32,1152]{2,1,0:T(8,128)(2,1)S(1)}, bf16[3,32,1152]{2,1,0:T(8,128)(2,1)S(1)}, u32[]{:S(2)}, u32[]{:S(2)}) %collective-permute-start.19) | collective-permute-done | bytes 221216 | tf_op jit(solution)/shard_map/ppermute | solution.py:24
  68.4 1.9 %line.3 = (bf16[8,32,1152]{2,1,0:T(8,128)(2,1)}, f32[32,1152]{1,0:T(8,128)S(1)}) custom-call(s32[1]{0:T(128)} %bitcast.2.z_ref, f32[3,32,1152]{2,1,0:T(8,128)S(1)} %get-tuple-element.112.refs_0_, bf16[3,32,1152]{2,1,0:T(8,128)(2,1)S(1)} %collective-permute-done.17.refs_1_, bf16[3,32,1152]{2,1,0:T(8,128)(2,1)S(1)} %collective-permute-done.18.refs_2_, ...), custom_call_target="tpu_custom_call" | custom-call | bytes 2580480 | tf_op jit(solution)/shard_map/line/pallas_call | solution.py:133
  70.3 3.5 %all-to-all-start = ((bf16[8,32,1152]{2,1,0:T(8,128)(2,1)}), bf16[8,32,1152]{2,1,0:T(8,128)(2,1)S(1)}, u32[]{:S(2)}, u32[]{:S(2)}) async-start(bf16[8,32,1152]{2,1,0:T(8,128)(2,1)} %get-tuple-element.127), calls=%async_computation | async-start | bytes 1179648 | tf_op jit(solution)/shard_map/all_to_all | solution.py:279
  76.0 11.8 %all-to-all-done.got_ref = bf16[8,32,1152]{2,1,0:T(8,128)(2,1)S(1)} async-done(((bf16[8,32,1152]{2,1,0:T(8,128)(2,1)}), bf16[8,32,1152]{2,1,0:T(8,128)(2,1)S(1)}, u32[]{:S(2)}, u32[]{:S(2)}) %all-to-all-start) | async-done | bytes 589856 | tf_op jit(solution)/shard_map/all_to_all | solution.py:279
  89.2 3.8 %all-to-all-start.1 = ((bf16[8,32,1024]{2,1,0:T(8,128)(2,1)}), bf16[8,32,1024]{2,1,0:T(8,128)(2,1)S(1)}, u32[]{:S(2)}, u32[]{:S(2)}) async-start(bf16[8,32,1024]{2,1,0:T(8,128)(2,1)} %finish.1), calls=%async_computation.1 | async-start | bytes 1048576 | tf_op jit(solution)/shard_map/all_to_all | solution.py:284
  93.0 12.9 %all-to-all-done.1.attn_ref = bf16[8,32,1024]{2,1,0:T(8,128)(2,1)S(1)} async-done(((bf16[8,32,1024]{2,1,0:T(8,128)(2,1)}), bf16[8,32,1024]{2,1,0:T(8,128)(2,1)S(1)}, u32[]{:S(2)}, u32[]{:S(2)}) %all-to-all-start.1) | async-done | bytes 524320 | tf_op jit(solution)/shard_map/all_to_all | solution.py:284
  113.1 2.4 %collective-permute-done.25 = bf16[128,256]{1,0:T(8,128)(2,1)S(1)} collective-permute-done((bf16[128,256]{1,0:T(8,128)(2,1)S(1)}, bf16[128,256]{1,0:T(8,128)(2,1)S(1)}, u32[]{:S(2)}, u32[]{:S(2)}) %collective-permute-start.25) | collective-permute-done | bytes 65568 | tf_op jit(solution)/shard_map/ppermute | solution.py:24
  116.7 2.1 %collective-permute-start.26 = (bf16[128,256]{1,0:T(8,128)(2,1)S(1)}, bf16[128,256]{1,0:T(8,128)(2,1)S(1)}, u32[]{:S(2)}, u32[]{:S(2)}) collective-permute-start(bf16[128,256]{1,0:T(8,128)(2,1)S(1)} %fusion.3), channel_id=1, source_target_pairs={{128,0},{192,24},{0,16},{64,8},{200,72},{8,64},{72,88},{136,80},{1... | collective-permute-start | bytes 196616 | tf_op jit(solution)/shard_map/ppermute | solution.py:303
  118.8 5.6 %collective-permute-done.26 = bf16[128,256]{1,0:T(8,128)(2,1)S(1)} collective-permute-done((bf16[128,256]{1,0:T(8,128)(2,1)S(1)}, bf16[128,256]{1,0:T(8,128)(2,1)S(1)}, u32[]{:S(2)}, u32[]{:S(2)}) %collective-permute-start.26) | collective-permute-done | bytes 65568 | tf_op jit(solution)/shard_map/ppermute | solution.py:303
  (60 shorter events, 34.2 us)
Async XLA Ops:
  5.5 6.2 %collective-permute-start = (bf16[32,1152]{1,0:T(8,128)(2,1)S(1)}, bf16[32,1152]{1,0:T(8,128)(2,1)S(1)}, u32[]{:S(2)}, u32[]{:S(2)}) collective-permute-start(bf16[32,1152]{1,0:T(8,128)(2,1)S(1)} %concatenate.3), channel_id=1, source_target_pairs={{0,8},{8,16},{16,24},{24,0},{1,9},{9,17},{17,25},{25,1},{2,10},{10... | collective-permute-start | bytes 221192 | tf_op jit(solution)/shard_map/ppermute | solution.py:24
  11.7 12.2 %collective-permute-start.4 = (bf16[4,32,1152]{2,1,0:T(8,128)(2,1)S(1)}, bf16[4,32,1152]{2,1,0:T(8,128)(2,1)S(1)}, u32[]{:S(2)}, u32[]{:S(2)}) collective-permute-start(bf16[4,32,1152]{2,1,0:T(8,128)(2,1)S(1)} %pad_maximum_fusion.refs_0_), channel_id=1, source_target_pairs={{0,7},{1,0},{2,1},{3,2},{4,3},{5,4},{6,5},{7,6},{8,15},{9,8},{10,9... | collective-permute-start | bytes 884744 | tf_op jit(solution)/shard_map/ppermute | solution.py:24
  17.6 8.5 %collective-permute-start.3 = (bf16[4,32,1152]{2,1,0:T(8,128)(2,1)S(1)}, bf16[4,32,1152]{2,1,0:T(8,128)(2,1)S(1)}, u32[]{:S(2)}, u32[]{:S(2)}) collective-permute-start(bf16[4,32,1152]{2,1,0:T(8,128)(2,1)S(1)} %pad_maximum_fusion.refs_0_), channel_id=1, source_target_pairs={{0,1},{1,2},{2,3},{3,4},{4,5},{5,6},{6,7},{7,0},{8,9},{9,10},{10,1... | collective-permute-start | bytes 884744 | tf_op jit(solution)/shard_map/ppermute | solution.py:24
  17.6 21.0 %collective-permute-start.9 = (bf16[1024,256]{1,0:T(8,128)(2,1)}, bf16[1024,256]{1,0:T(8,128)(2,1)S(1)}, u32[]{:S(2)}, u32[]{:S(2)}) collective-permute-start(bf16[1024,256]{1,0:T(8,128)(2,1)} %refs_0_), channel_id=1, source_target_pairs={{0,16},{8,24},{16,0},{24,8},{1,17},{9,25},{17,1},{25,9},{2,18},{10... | collective-permute-start | bytes 1572872 | tf_op jit(solution)/shard_map/ppermute | solution.py:24
  26.1 7.9 %collective-permute-start.5 = (bf16[4,32,1152]{2,1,0:T(8,128)(2,1)S(1)}, bf16[4,32,1152]{2,1,0:T(8,128)(2,1)S(1)}, u32[]{:S(2)}, u32[]{:S(2)}) collective-permute-start(bf16[4,32,1152]{2,1,0:T(8,128)(2,1)S(1)} %collective-permute-done.3.refs_0_), channel_id=1, source_target_pairs={{0,1},{1,2},{2,3},{3,4},{4,5},{5,6},{6,7},{7,0},{8,9},{9,10},{10,1... | collective-permute-start | bytes 884744 | tf_op jit(solution)/shard_map/ppermute | solution.py:24
  26.1 7.9 %collective-permute-start.6 = (bf16[4,32,1152]{2,1,0:T(8,128)(2,1)S(1)}, bf16[4,32,1152]{2,1,0:T(8,128)(2,1)S(1)}, u32[]{:S(2)}, u32[]{:S(2)}) collective-permute-start(bf16[4,32,1152]{2,1,0:T(8,128)(2,1)S(1)} %collective-permute-done.4.refs_1_), channel_id=1, source_target_pairs={{0,7},{1,0},{2,1},{3,2},{4,3},{5,4},{6,5},{7,6},{8,15},{9,8},{10,9... | collective-permute-start | bytes 884744 | tf_op jit(solution)/shard_map/ppermute | solution.py:24
  34.1 9.5 %collective-permute-start.7 = (bf16[4,32,1152]{2,1,0:T(8,128)(2,1)S(1)}, bf16[4,32,1152]{2,1,0:T(8,128)(2,1)S(1)}, u32[]{:S(2)}, u32[]{:S(2)}) collective-permute-start(bf16[4,32,1152]{2,1,0:T(8,128)(2,1)S(1)} %collective-permute-done.5.refs_0_), channel_id=1, source_target_pairs={{0,1},{1,2},{2,3},{3,4},{4,5},{5,6},{6,7},{7,0},{8,9},{9,10},{10,1... | collective-permute-start | bytes 884744 | tf_op jit(solution)/shard_map/ppermute | solution.py:24
  34.1 9.5 %collective-permute-start.8 = (bf16[4,32,1152]{2,1,0:T(8,128)(2,1)S(1)}, bf16[4,32,1152]{2,1,0:T(8,128)(2,1)S(1)}, u32[]{:S(2)}, u32[]{:S(2)}) collective-permute-start(bf16[4,32,1152]{2,1,0:T(8,128)(2,1)S(1)} %collective-permute-done.6.refs_1_), channel_id=1, source_target_pairs={{0,7},{1,0},{2,1},{3,2},{4,3},{5,4},{6,5},{7,6},{8,15},{9,8},{10,9... | collective-permute-start | bytes 884744 | tf_op jit(solution)/shard_map/ppermute | solution.py:24
  37.3 8.4 %collective-permute-start.11 = (bf16[3,32,1152]{2,1,0:T(8,128)(2,1)S(1)}, bf16[3,32,1152]{2,1,0:T(8,128)(2,1)S(1)}, u32[]{:S(2)}, u32[]{:S(2)}) collective-permute-start(bf16[3,32,1152]{2,1,0:T(8,128)(2,1)S(1)} %get-tuple-element.93), channel_id=1, source_target_pairs={{0,24},{8,0},{16,8},{24,16},{1,25},{9,1},{17,9},{25,17},{2,26},{10... | collective-permute-start | bytes 663560 | tf_op jit(solution)/shard_map/ppermute | solution.py:24
  37.9 9.4 %collective-permute-start.12 = (bf16[3,32,1152]{2,1,0:T(8,128)(2,1)S(1)}, bf16[3,32,1152]{2,1,0:T(8,128)(2,1)S(1)}, u32[]{:S(2)}, u32[]{:S(2)}) collective-permute-start(bf16[3,32,1152]{2,1,0:T(8,128)(2,1)S(1)} %get-tuple-element.94), channel_id=1, source_target_pairs={{0,16},{8,24},{16,0},{24,8},{1,17},{9,25},{17,1},{25,9},{2,18},{10... | collective-permute-start | bytes 663560 | tf_op jit(solution)/shard_map/ppermute | solution.py:24
  38.6 12.2 %collective-permute-start.13 = (bf16[3,32,1152]{2,1,0:T(8,128)(2,1)S(1)}, bf16[3,32,1152]{2,1,0:T(8,128)(2,1)S(1)}, u32[]{:S(2)}, u32[]{:S(2)}) collective-permute-start(bf16[3,32,1152]{2,1,0:T(8,128)(2,1)S(1)} %get-tuple-element.95), channel_id=1, source_target_pairs={{0,8},{8,16},{16,24},{24,0},{1,9},{9,17},{17,25},{25,1},{2,10},{10... | collective-permute-start | bytes 663560 | tf_op jit(solution)/shard_map/ppermute | solution.py:24
  43.6 11.1 %collective-permute-start.10 = (bf16[4,32,1152]{2,1,0:T(8,128)(2,1)S(1)}, bf16[4,32,1152]{2,1,0:T(8,128)(2,1)S(1)}, u32[]{:S(2)}, u32[]{:S(2)}) collective-permute-start(bf16[4,32,1152]{2,1,0:T(8,128)(2,1)S(1)} %collective-permute-done.7.refs_0_), channel_id=1, source_target_pairs={{0,1},{1,2},{2,3},{3,4},{4,5},{5,6},{6,7},{7,0},{8,9},{9,10},{10,1... | collective-permute-start | bytes 884744 | tf_op jit(solution)/shard_map/ppermute | solution.py:24
  43.7 10.7 %collective-permute-start.14 = (bf16[2,32,1152]{2,1,0:T(8,128)(2,1)S(1)}, bf16[2,32,1152]{2,1,0:T(8,128)(2,1)S(1)}, u32[]{:S(2)}, u32[]{:S(2)}) collective-permute-start(bf16[2,32,1152]{2,1,0:T(8,128)(2,1)S(1)} %get-tuple-element.103), channel_id=1, source_target_pairs={{0,24},{8,0},{16,8},{24,16},{1,25},{9,1},{17,9},{25,17},{2,26},{10... | collective-permute-start | bytes 442376 | tf_op jit(solution)/shard_map/ppermute | solution.py:24
  45.7 8.7 %collective-permute-start.15 = (bf16[2,32,1152]{2,1,0:T(8,128)(2,1)S(1)}, bf16[2,32,1152]{2,1,0:T(8,128)(2,1)S(1)}, u32[]{:S(2)}, u32[]{:S(2)}) collective-permute-start(bf16[2,32,1152]{2,1,0:T(8,128)(2,1)S(1)} %get-tuple-element.104), channel_id=1, source_target_pairs={{0,16},{8,24},{16,0},{24,8},{1,17},{9,25},{17,1},{25,9},{2,18},{10... | collective-permute-start | bytes 442376 | tf_op jit(solution)/shard_map/ppermute | solution.py:24
  47.3 7.4 %collective-permute-start.16 = (bf16[2,32,1152]{2,1,0:T(8,128)(2,1)S(1)}, bf16[2,32,1152]{2,1,0:T(8,128)(2,1)S(1)}, u32[]{:S(2)}, u32[]{:S(2)}) collective-permute-start(bf16[2,32,1152]{2,1,0:T(8,128)(2,1)S(1)} %get-tuple-element.105), channel_id=1, source_target_pairs={{0,8},{8,16},{16,24},{24,0},{1,9},{9,17},{17,25},{25,1},{2,10},{10... | collective-permute-start | bytes 442376 | tf_op jit(solution)/shard_map/ppermute | solution.py:24
  56.8 8.0 %collective-permute-start.17 = (bf16[3,32,1152]{2,1,0:T(8,128)(2,1)S(1)}, bf16[3,32,1152]{2,1,0:T(8,128)(2,1)S(1)}, u32[]{:S(2)}, u32[]{:S(2)}) collective-permute-start(bf16[3,32,1152]{2,1,0:T(8,128)(2,1)S(1)} %get-tuple-element.113), channel_id=1, source_target_pairs={{0,24},{8,0},{16,8},{24,16},{1,25},{9,1},{17,9},{25,17},{2,26},{10... | collective-permute-start | bytes 663560 | tf_op jit(solution)/shard_map/ppermute | solution.py:24
  58.9 7.5 %collective-permute-start.18 = (bf16[3,32,1152]{2,1,0:T(8,128)(2,1)S(1)}, bf16[3,32,1152]{2,1,0:T(8,128)(2,1)S(1)}, u32[]{:S(2)}, u32[]{:S(2)}) collective-permute-start(bf16[3,32,1152]{2,1,0:T(8,128)(2,1)S(1)} %get-tuple-element.114), channel_id=1, source_target_pairs={{0,16},{8,24},{16,0},{24,8},{1,17},{9,25},{17,1},{25,9},{2,18},{10... | collective-permute-start | bytes 663560 | tf_op jit(solution)/shard_map/ppermute | solution.py:24
  58.9 9.5 %collective-permute-start.19 = (bf16[3,32,1152]{2,1,0:T(8,128)(2,1)S(1)}, bf16[3,32,1152]{2,1,0:T(8,128)(2,1)S(1)}, u32[]{:S(2)}, u32[]{:S(2)}) collective-permute-start(bf16[3,32,1152]{2,1,0:T(8,128)(2,1)S(1)} %get-tuple-element.115), channel_id=1, source_target_pairs={{0,8},{8,16},{16,24},{24,0},{1,9},{9,17},{17,25},{25,1},{2,10},{10... | collective-permute-start | bytes 663560 | tf_op jit(solution)/shard_map/ppermute | solution.py:24
  70.3 17.5 %all-to-all-start = ((bf16[8,32,1152]{2,1,0:T(8,128)(2,1)}), bf16[8,32,1152]{2,1,0:T(8,128)(2,1)S(1)}, u32[]{:S(2)}, u32[]{:S(2)}) async-start(bf16[8,32,1152]{2,1,0:T(8,128)(2,1)} %get-tuple-element.127), calls=%async_computation | async-start | bytes 1179648 | tf_op jit(solution)/shard_map/all_to_all | solution.py:279
  73.9 15.3 %collective-permute-start.21 = (bf16[1024,256]{1,0:T(8,128)(2,1)S(1)}, bf16[1024,256]{1,0:T(8,128)(2,1)S(1)}, u32[]{:S(2)}, u32[]{:S(2)}) collective-permute-start(bf16[1024,256]{1,0:T(8,128)(2,1)S(1)} %copy-done.3), channel_id=1, source_target_pairs={{0,24},{8,0},{16,8},{24,16},{1,25},{9,1},{17,9},{25,17},{2,26},{10... | collective-permute-start | bytes 1572872 | tf_op jit(solution)/shard_map/ppermute | solution.py:24
  74.9 14.3 %collective-permute-start.20 = (bf16[1024,256]{1,0:T(8,128)(2,1)S(1)}, bf16[1024,256]{1,0:T(8,128)(2,1)S(1)}, u32[]{:S(2)}, u32[]{:S(2)}) collective-permute-start(bf16[1024,256]{1,0:T(8,128)(2,1)S(1)} %copy-done.3), channel_id=1, source_target_pairs={{0,8},{8,16},{16,24},{24,0},{1,9},{9,17},{17,25},{25,1},{2,10},{10... | collective-permute-start | bytes 1572872 | tf_op jit(solution)/shard_map/ppermute | solution.py:24
  89.2 16.7 %all-to-all-start.1 = ((bf16[8,32,1024]{2,1,0:T(8,128)(2,1)}), bf16[8,32,1024]{2,1,0:T(8,128)(2,1)S(1)}, u32[]{:S(2)}, u32[]{:S(2)}) async-start(bf16[8,32,1024]{2,1,0:T(8,128)(2,1)} %finish.1), calls=%async_computation.1 | async-start | bytes 1048576 | tf_op jit(solution)/shard_map/all_to_all | solution.py:284
  109.3 6.2 %collective-permute-start.25 = (bf16[128,256]{1,0:T(8,128)(2,1)S(1)}, bf16[128,256]{1,0:T(8,128)(2,1)S(1)}, u32[]{:S(2)}, u32[]{:S(2)}) collective-permute-start(bf16[128,256]{1,0:T(8,128)(2,1)S(1)} %get-tuple-element.138), channel_id=1, source_target_pairs={{0,192},{64,0},{128,64},{192,128},{1,193},{65,1},{129,65},{193,129... | collective-permute-start | bytes 196616 | tf_op jit(solution)/shard_map/ppermute | solution.py:24
  116.7 7.7 %collective-permute-start.26 = (bf16[128,256]{1,0:T(8,128)(2,1)S(1)}, bf16[128,256]{1,0:T(8,128)(2,1)S(1)}, u32[]{:S(2)}, u32[]{:S(2)}) collective-permute-start(bf16[128,256]{1,0:T(8,128)(2,1)S(1)} %fusion.3), channel_id=1, source_target_pairs={{128,0},{192,24},{0,16},{64,8},{200,72},{8,64},{72,88},{136,80},{1... | collective-permute-start | bytes 196616 | tf_op jit(solution)/shard_map/ppermute | solution.py:303
  (9 other events, 57.4 us)
